TPU v7x, 256 devices: a whole 4x4x8 slice. The times are simulated.
256 devices in a mesh: row: 16 (over z, y_hi), col: 4 (over x), depth: 4 (over y_lo, core).
Axes of the slice: x: 4, y: 4 (y_hi: 2, y_lo: 2; y = y_hi * 2 + y_lo), z: 8, core: 2. Of those that a mesh axis runs over, the one named last changes fastest.
Arguments:
- integrals: bfloat16 [16384, 5120], P('row', 'depth'), may hold values from -0.25 to 0.25
- amplitudes: bfloat16 [160, 32, 10000], P('depth', 'row', 'col'), may hold values from -6 to 6
- ab_irrep: int32 [16384], P('row'), may hold values from 0 to 7
- cd_irrep: int32 [5120], P('depth'), may hold values from 0 to 7
Outputs:
- residual: bfloat16 [16384, 10000], P(('row', 'depth'), 'col')
All inputs are finite; a program needn't handle non-finite values.
Results may differ from a plain program's by a relative error of at most 0.001.
Values may be sent and summed in bfloat16 or wider, within the bound.
A program may use at most 192 MiB of HBM per device.

v0:
```python
import jax
import jax.numpy as jnp
from jax import lax
from jax.sharding import PartitionSpec as P

OCC = 100


def local(integrals, amplitudes, ab_irrep, cd_irrep):
    keep = ab_irrep[:, None] == cd_irrep[None, :]
    masked = jnp.where(keep, integrals, jnp.zeros_like(integrals))
    rows_here = masked.shape[0]
    blocks_here = amplitudes.shape[0]
    sub_here = amplitudes.shape[1]
    columns = amplitudes.shape[2]
    sub_full = sub_here * lax.axis_size("row")
    shaped = masked.reshape(rows_here, blocks_here, sub_full)
    total = jnp.einsum(
        "rck,ckj->rj",
        shaped,
        lax.all_gather(amplitudes, "row", axis=1, tiled=True),
        preferred_element_type=jnp.float32,
    )
    ladder = lax.psum_scatter(total, "depth", scatter_dimension=0, tiled=True)
    out_rows = ladder.shape[0]
    local_occ = columns // OCC
    cube = ladder.reshape(out_rows, local_occ, OCC)
    mirrored = lax.all_to_all(cube, "col", split_axis=2, concat_axis=1, tiled=True)
    result = cube - jnp.swapaxes(mirrored, 1, 2)
    return result.reshape(out_rows, columns).astype(jnp.bfloat16)


def solution(mesh):
    in_specs = (P("row", "depth"), P("depth", "row", "col"), P("row"), P("depth"))
    out_specs = P(("row", "depth"), "col")
    return jax.shard_map(local, mesh=mesh, in_specs=in_specs, out_specs=out_specs, check_vma=False)
```

profile of v0, /device:TPU:1, one launch (start us, length us, event | category | flops | bytes accessed | tf_op | source)
XLA Modules:
  0.0 303.1 jit_solution(9529771054664287746)
XLA Ops:
  6.5 0.0 all-gather.2.cloned.1.call-start
  6.5 1.8 copy.13
  8.3 0.0 all-gather.2.cloned.1.call-update
  8.4 0.0 copy-start
  8.4 0.0 copy-start.1
  8.4 0.0 reduce-scatter.2.cloned.1.call-start
  8.4 3.0 copy.12
  11.4 0.0 copy-done
  11.4 0.0 copy-done.1
  11.5 2.2 compare_select_fusion
  13.6 117.7 %all-gather.2.cloned.1.call-done = bf16[40,32,2500]{2,0,1:T(8,128)(2,1)} async-done(((bf16[40,2,2500]{2,0,1:T(8,128)(2,1)}), bf16[40,32,2500]{2,0,1:T(8,128)(2,1)}) %all-gather.2.cloned.1.call-update) | async-done | bytes 6400016 | tf_op jit(solution)/shard_map/all_gather | solution.py:21
  131.3 12.8 %fusion.2 = f32[1024,2500]{0,1:T(8,128)} fusion(bf16[1024,40,32]{0,2,1:T(8,128)(2,1)} %bitcast.19, bf16[40,32,2500]{2,0,1:T(8,128)(2,1)} %all-gather.2.cloned.1.call-done), kind=kOutput, calls=%fused_computation.2 | convolution fusion | flops 6553600000 | bytes 19261440 | tf_op jit(solution)/shard_map/rck,ckj->rj/dot_general | solution.py:18
  144.2 0.0 reduce-scatter.2.cloned.1.call-update
  144.2 94.7 %reduce-scatter.2.cloned.1.call-done = f32[256,2500]{0,1:T(8,128)} async-done(((f32[1024,2500]{0,1:T(8,128)}), f32[256,2500]{0,1:T(8,128)}) %reduce-scatter.2.cloned.1.call-update) | async-done | bytes 2560016 | tf_op jit(solution)/shard_map/reduce_scatter | solution.py:24
  238.9 2.4 reshape.11
  241.3 0.9 copy.15
  242.2 41.8 %all_to_all.18 = f32[256,25,100]{0,1,2:T(8,128)S(1)} all-to-all(f32[256,25,100]{0,1,2:T(8,128)S(1)} %copy.15), channel_id=1, replica_groups=mesh['row'=16,'col'=4,'depth'=4] {'col'}, dimensions={2} | all-to-all | bytes 5120000 | tf_op jit(solution)/shard_map/all_to_all | solution.py:28
  284.1 1.9 copy.17
  286.0 4.4 %all_to_all.16 = f32[256,100,25]{0,1,2:T(8,128)} reshape(f32[256,4,25,25]{0,2,1,3:T(8,128)} %copy.17) | data formatting | bytes 5120000 | tf_op jit(solution)/shard_map/all_to_all | solution.py:28
  290.3 3.2 %fusion.5 = bf16[256,25,100]{0,2,1:T(8,128)(2,1)} fusion(f32[256,25,100]{0,2,1:T(8,128)S(1)} %reshape.11, f32[256,100,25]{0,1,2:T(8,128)} %all_to_all.16), kind=kLoop, calls=%fused_computation.5 | loop fusion | flops 1280000 | bytes 6400000 | tf_op jit(solution)/shard_map/convert_element_type | solution.py:30
  293.6 2.7 convert_element_type.7
Async XLA Ops:
  6.5 124.8 %all-gather.2.cloned.1.call-start = ((), (), s32[]{:S(2)}) async-start(), calls=%async_computation.2 | async-start | bytes 6963200 | tf_op jit(solution)/shard_map/all_gather | solution.py:21
  8.4 3.1 %copy-start = (s32[1280]{0:T(1024)S(1)}, s32[1280]{0:T(1024)}, u32[]{:S(2)}) copy-start(s32[1280]{0:T(1024)} %param.7) | copy-start | bytes 15364
  8.4 3.1 %copy-start.1 = (s32[1024]{0:T(1024)S(1)}, s32[1024]{0:T(1024)}, u32[]{:S(2)}) copy-start(s32[1024]{0:T(1024)} %param.6) | copy-start | bytes 12292
  8.4 230.5 %reduce-scatter.2.cloned.1.call-start = ((), (), s32[]{:S(2)}) async-start(), calls=%async_computation.3 | async-start | bytes 12820480 | tf_op jit(solution)/shard_map/reduce_scatter | solution.py:24
Sparse Core Ops, SparseCore 0:
  9.9 121.3 all-gather.1
  144.3 94.5 reduce-scatter.1
where the time goes:
time: 304 us; the launch traced here: 303 us
  waiting for transfers between devices  212 us (70%)
  blocking collectives  41.8 us (14%)
  local copies, waits for them, and re-layouts  17 us (6%)
  between operations  13.4 us (4%)
  matrix products  12.8 us (4%)
  other arithmetic  5.42 us (2%)
    all_gather x1, waiting for transfers between devices, local(): lax.all_gather(amplitudes, 'row', axis=1, tiled=True)  118 us
    reduce_scatter x1, waiting for transfers between devices, local(): ladder = lax.psum_scatter(total, 'depth', scatter_dimension=0, tiled=True)  94.7 us
    all_to_all x1, blocking collectives, local(): lax.all_to_all(cube, 'col', split_axis=2, concat_axis=1, tiled=True)  41.8 us
    dot_general x1, matrix products, local(): jnp.einsum('rck,ckj->rj', shaped, lax.all_gather(amplitudes, 'row', axis=...  12.8 us
    all_to_all x2, local copies, waits for them, and re-layouts, local(): lax.all_to_all(cube, 'col', split_axis=2, concat_axis=1, tiled=True)  6.28 us
  transfers between devices with their start and end apart: 2, of which 2 were waited for; matrix products, arithmetic and copies ran while one was open for 2% of the time, Pallas kernels for 0%

commit v1 on v0

v1 whole, which is shorter than its diff:
```python
import numpy as np

import jax
import jax.numpy as jnp
from jax import lax
from jax.experimental import pallas as pl
from jax.experimental.pallas import tpu as pltpu
from jax.sharding import PartitionSpec as P

OCC = 100
SUB = 25
NZ = 8
LANES = 128
CHUNKS = 10
HALF = 640
PAD = 15
PAIRS = CHUNKS * LANES
ROWS_T = 80
DEPTH = 1280
OUT_ROWS = 256
WIDE = 2560
MESH = pl.DeviceIdType.MESH


def iota(shape, dim):
    return lax.broadcasted_iota(jnp.int32, shape, dim)


def div25(v):
    return (v * 5243) >> 17


def div100(v):
    return (v * 5243) >> 19


def one_hot(cond):
    return jnp.where(cond, 1.0, 0.0).astype(jnp.bfloat16)


def dot(a, b):
    return jnp.dot(a, b, preferred_element_type=jnp.float32)


def band(n):
    lanes = np.arange(n * LANES, (n + 1) * LANES) - PAD
    lanes = lanes[(lanes >= 0) & (lanes < SUB * SUB)]
    first = 100 * (lanes // SUB) + lanes % SUB
    low = first.min() // LANES * LANES
    high = -(-(first.max() + 76) // LANES) * LANES
    return int(low), int(min(high, WIDE))


def kernel(
    t_ref, ab_ref, cd_ref, v_hbm, out_ref,
    v_ref, vp_ref, pk_ref, pt_ref, x_ref, wsend, wrecv, bq, sc_ref, bhl,
    csend, crecv, ysend, yrecv, own, r_own, r_recv, g_ref, src_ref, sgn_ref, acc_ref,
    v_sem, w_ss, w_rs, h_ss, h_rs, zr_ss, zr_rs, zl_ss, zl_rs, c_ss, c_rs, y_ss, y_rs, m_ss, m_rs,
):
    row, c, depth = lax.axis_index("row"), lax.axis_index("col"), lax.axis_index("depth")
    z, yh = row // 2, row % 2
    yl, core = depth // 2, depth % 2
    d_right = ((row + 2) % 16, c, depth)
    d_left = ((row + 14) % 16, c, depth)
    d_hi = (2 * z + 1 - yh, c, depth)
    d_core = (row, c, 2 * yl + 1 - core)
    d_lo = (row, c, 2 * (1 - yl) + core)
    x_next = (row, (c + 1) % 4, depth)
    x_opp = (row, (c + 2) % 4, depth)
    x_prev = (row, (c + 3) % 4, depth)

    def copy(src, dst, ss, rs, dev):
        return pltpu.make_async_remote_copy(
            src_ref=src, dst_ref=dst, send_sem=ss, recv_sem=rs, device_id=dev, device_id_type=MESH
        )

    v_copy = pltpu.make_async_copy(v_hbm, v_ref, v_sem)
    v_copy.start()

    barrier = pltpu.get_barrier_semaphore()
    for dev in (d_right, d_left, d_hi, d_core, d_lo, x_next, x_opp, x_prev):
        pl.semaphore_signal(barrier, inc=1, device_id=dev, device_id_type=MESH)

    u = iota((1, HALF), 1) - PAD
    a = div25(u)
    b = u - SUB * a
    flip = jnp.where(u >= 0, PAD + SUB * b + a, -1)
    lower = b <= a
    pt_ref[...] = one_hot(iota((HALF, HALF), 0) == flip)

    for n in range(HALF // LANES):
        low, high = band(n)
        u = iota((1, LANES), 1) + (n * LANES - PAD)
        a = div25(u)
        first = 100 * a + (u - SUB * a)
        r = iota((high - low, LANES), 0) + low
        mats = []
        for g in range(4):
            want = jnp.where((u >= 0), first + SUB * ((c + g) % 4), -1)
            mats.append(one_hot(r == want))
        got = dot(t_ref[:, low:high], jnp.concatenate(mats, axis=1)).astype(jnp.bfloat16)
        for g in range(4):
            x_ref[g, :, n * LANES:(n + 1) * LANES] = got[:, g * LANES:(g + 1) * LANES]

    wsend[0] = dot(x_ref[3], pt_ref[...]).astype(jnp.bfloat16)
    wsend[1] = dot(x_ref[2], pt_ref[...]).astype(jnp.bfloat16)
    pl.semaphore_wait(barrier, 8)
    w0 = copy(wsend.at[0], wrecv.at[0], w_ss.at[0], w_rs.at[0], x_prev)
    w1 = copy(wsend.at[1], wrecv.at[1], w_ss.at[1], w_rs.at[1], x_opp)
    w1.start()
    w0.start()
    x0 = x_ref[0]
    diag = x0.astype(jnp.float32) - dot(x0, pt_ref[...])

    k = iota((1, DEPTH), 1)
    zz = (k * 3277) >> 19
    rem = k - 160 * zz
    hh = jnp.where(rem >= 80, 1, 0)
    m = rem - 80 * hh
    from_k = 32 * (m >> 1) + 4 * zz + 2 * hh + (m & 1)

    def make_pk(i, _):
        base = pl.multiple_of(i * 256, 256)
        pk_ref[pl.ds(base, 256), :] = one_hot(iota((256, DEPTH), 0) + base == from_k)
        return 0

    lax.fori_loop(0, DEPTH // 256, make_pk, 0)
    v_copy.wait()

    def make_vp(i, _):
        base = pl.multiple_of(i * 128, 128)
        rows = pl.ds(base, 128)
        keep = ab_ref[rows, :] == cd_ref[...]
        masked = jnp.where(keep, v_ref[rows, :].astype(jnp.float32), 0.0).astype(jnp.bfloat16)
        vp_ref[rows, :] = dot(masked, pk_ref[...]).astype(jnp.bfloat16)
        return 0

    lax.fori_loop(0, 8, make_vp, 0)

    w0.wait_recv()
    w1.wait_recv()
    ta1 = x_ref[1].astype(jnp.float32) - wrecv[0].astype(jnp.float32)
    ta2 = jnp.where(lower, x_ref[2].astype(jnp.float32) - wrecv[1].astype(jnp.float32), diag)
    biggest = jnp.maximum(
        jnp.max(jnp.abs(ta1), axis=1, keepdims=True), jnp.max(jnp.abs(ta2), axis=1, keepdims=True)
    )
    exponent = jnp.ceil(jnp.log2(jnp.maximum(biggest, 1e-30))) - 15.0
    scale = jnp.exp2(-exponent)

    def coded(v):
        return jnp.clip(jnp.floor(v * scale + 0.5), -32767.0, 32767.0)

    q2 = coded(ta2)
    q1 = coded(ta1)
    q2 = jnp.where(iota((ROWS_T, HALF), 1) < PAD, jnp.broadcast_to(exponent, (ROWS_T, HALF)), q2)
    for n in range(CHUNKS):
        q = q2 if n < 5 else q1
        part = q[:, (n % 5) * LANES:(n % 5 + 1) * LANES]
        bq[n, z, yh] = part.astype(jnp.int32).astype(jnp.int16)

    def hi_copy(n):
        return copy(bq.at[n, z, yh], bq.at[n, z, yh], h_ss.at[n], h_rs.at[n], d_hi)

    def right_copy(n, s):
        at = (z - s + NZ) % NZ
        return copy(bq.at[n, at], bq.at[n, at], zr_ss.at[n, s], zr_rs.at[n, s], d_right)

    def left_copy(n, s):
        at = (z + s) % NZ
        return copy(bq.at[n, at], bq.at[n, at], zl_ss.at[n, s], zl_rs.at[n, s], d_left)

    def right_last(n):
        at = (z - 3 + NZ) % NZ
        return copy(bq.at[n, at, 0], bq.at[n, at, 0], zr_ss.at[n, 3], zr_rs.at[n, 3], d_right)

    def left_last(n):
        at = (z + 3) % NZ
        return copy(bq.at[n, at, 1], bq.at[n, at, 1], zl_ss.at[n, 3], zl_rs.at[n, 3], d_left)

    def core_copy(n, h):
        return copy(csend.at[n, h], crecv.at[n, h], c_ss.at[n, h], c_rs.at[n, h], d_core)

    def lo_copy(n):
        return copy(ysend.at[n], yrecv.at[n], y_ss.at[n], y_rs.at[n], d_lo)

    def mirror_copy(n):
        to = (row, (c + 2 - n // 5) % 4, depth)
        return copy(r_own.at[n], r_recv.at[n], m_ss.at[n], m_rs.at[n], to)

    hi_copy(0).start()
    hi_copy(1).start()

    lane = iota((1, WIDE), 1)
    a = div100(lane)
    j = lane - OCC * a
    grp = div25(j)
    b = j - SUB * grp
    rel = (grp - c + 4) % 4
    direct = PAD + SUB * a + b
    turned = PAD + SUB * b + a
    src = jnp.where(
        rel == 0,
        jnp.where(b > a, direct, jnp.where(b < a, turned, -1)),
        jnp.where(
            rel == 1,
            HALF + direct,
            jnp.where(rel == 2, jnp.where(b <= a, direct, 2048 + turned), 2048 + HALF + turned),
        ),
    )
    src_ref[...] = jnp.where(lane < OCC * SUB, src, -1)
    minus = ((rel == 0) & (b < a)) | ((rel == 2) & (b > a)) | (rel == 3)
    sgn_ref[...] = jnp.where(minus, -1.0, 1.0)
    acc_ref[...] = jnp.zeros_like(acc_ref)

    def block(yl_at, core_at):
        at = pl.multiple_of((2 * yl_at + core_at) * OUT_ROWS, OUT_ROWS)
        both = dot(vp_ref[pl.ds(at, OUT_ROWS), :], bhl[...])
        return both[:, :LANES] + both[:, LANES:]

    def step(t, _):
        n4 = t - 3

        @pl.when((n4 >= 0) & (n4 < CHUNKS))
        def _():
            right_copy(n4, 2).wait_recv()
            right_last(n4).start()
            left_copy(n4, 2).wait_recv()
            left_last(n4).start()

        n3 = t - 2

        @pl.when((n3 >= 0) & (n3 < CHUNKS))
        def _():
            right_copy(n3, 1).wait_recv()
            right_copy(n3, 2).start()
            left_copy(n3, 1).wait_recv()
            left_copy(n3, 2).start()

        n2 = t - 1

        @pl.when((n2 >= 0) & (n2 < CHUNKS))
        def _():
            right_copy(n2, 0).wait_recv()
            right_copy(n2, 1).start()
            left_copy(n2, 0).wait_recv()
            left_copy(n2, 1).start()

        @pl.when(t + 2 < CHUNKS)
        def _():
            hi_copy(t + 2).start()

        @pl.when(t < CHUNKS)
        def _():
            hi_copy(t).wait_recv()
            right_copy(t, 0).start()
            left_copy(t, 0).start()

        n = t - 4

        @pl.when((n >= 0) & (n < CHUNKS))
        def _():
            right_last(n).wait_recv()
            left_last(n).wait_recv()
            q = bq[n].reshape(DEPTH, LANES).astype(jnp.int32)

            @pl.when(n == 0)
            def _():
                sc_ref[...] = jnp.broadcast_to(jnp.exp2(q[:, 0:1].astype(jnp.float32)), (DEPTH, LANES))

            s = sc_ref[...]
            hi = (q + 128) >> 8
            lo = q - (hi << 8)
            bhl[:, :LANES] = (hi.astype(jnp.float32) * (s * 256.0)).astype(jnp.bfloat16)
            bhl[:, LANES:] = (lo.astype(jnp.float32) * s).astype(jnp.bfloat16)
            csend[n, 0] = block(1 - yl, 1 - core)
            core_copy(n, 0).start()
            csend[n, 1] = block(yl, 1 - core)
            core_copy(n, 1).start()
            part = block(1 - yl, core)
            core_copy(n, 0).wait_recv()
            ysend[n] = part + crecv[n, 0]
            lo_copy(n).start()
            part = block(yl, core)
            core_copy(n, 1).wait_recv()
            own[n] = part + crecv[n, 1]

        f = t - 5

        @pl.when((f >= 0) & (f < CHUNKS))
        def _():
            lo_copy(f).wait_recv()
            r_own[f] = (own[f] + yrecv[f]).astype(jnp.bfloat16)
            mirror_copy(f).start()

        @pl.when(t < CHUNKS)
        def _():
            r = iota((2 * LANES, 512), 0)
            r = r + (t * LANES + jnp.where(r >= LANES, 2048 - LANES, 0))
            for w in range(WIDE // 512):
                at = slice(w * 512, (w + 1) * 512)
                g_ref[t, :, at] = jnp.where(r == src_ref[:, at], sgn_ref[:, at], 0.0).astype(jnp.bfloat16)

        h = t - 6

        @pl.when((h >= 0) & (h < CHUNKS))
        def _():
            mirror_copy(h).wait_recv()
            both = jnp.concatenate([r_own[h], r_recv[h]], axis=1)
            for w in range(WIDE // 512):
                at = slice(w * 512, (w + 1) * 512)
                acc_ref[:, at] += dot(both, g_ref[h, :, at])

        return 0

    lax.fori_loop(0, CHUNKS + 6, step, 0)
    out_ref[...] = acc_ref[:, : OCC * SUB].astype(jnp.bfloat16)

    w0.wait_send()
    w1.wait_send()

    def drain(n, _):
        hi_copy(n).wait_send()
        for s in range(3):
            right_copy(n, s).wait_send()
            left_copy(n, s).wait_send()
        right_last(n).wait_send()
        left_last(n).wait_send()
        core_copy(n, 0).wait_send()
        core_copy(n, 1).wait_send()
        lo_copy(n).wait_send()
        mirror_copy(n).wait_send()
        return 0

    lax.fori_loop(0, CHUNKS, drain, 0)


def local(integrals, amplitudes, ab_irrep, cd_irrep):
    amps = jnp.pad(amplitudes.reshape(ROWS_T, OCC * SUB), ((0, 0), (0, WIDE - OCC * SUB)))
    vmem = pl.BlockSpec(memory_space=pltpu.VMEM)
    bf, f32 = jnp.bfloat16, jnp.float32
    dma = pltpu.SemaphoreType.DMA
    n = CHUNKS
    scratch = [
        pltpu.VMEM((1024, DEPTH), bf),
        pltpu.VMEM((1024, DEPTH), bf),
        pltpu.VMEM((DEPTH, DEPTH), bf),
        pltpu.VMEM((HALF, HALF), bf),
        pltpu.VMEM((4, ROWS_T, HALF), bf),
        pltpu.VMEM((2, ROWS_T, HALF), bf),
        pltpu.VMEM((2, ROWS_T, HALF), bf),
        pltpu.VMEM((n, NZ, 2, ROWS_T, LANES), jnp.int16),
        pltpu.VMEM((DEPTH, LANES), f32),
        pltpu.VMEM((DEPTH, 2 * LANES), bf),
        pltpu.VMEM((n, 2, OUT_ROWS, LANES), f32),
        pltpu.VMEM((n, 2, OUT_ROWS, LANES), f32),
        pltpu.VMEM((n, OUT_ROWS, LANES), f32),
        pltpu.VMEM((n, OUT_ROWS, LANES), f32),
        pltpu.VMEM((n, OUT_ROWS, LANES), f32),
        pltpu.VMEM((n, OUT_ROWS, LANES), bf),
        pltpu.VMEM((n, OUT_ROWS, LANES), bf),
        pltpu.VMEM((n, 2 * LANES, WIDE), bf),
        pltpu.VMEM((1, WIDE), jnp.int32),
        pltpu.VMEM((1, WIDE), f32),
        pltpu.VMEM((OUT_ROWS, WIDE), f32),
        dma,
        dma((2,)), dma((2,)),
        dma((n,)), dma((n,)),
        dma((n, 4)), dma((n, 4)),
        dma((n, 4)), dma((n, 4)),
        dma((n, 2)), dma((n, 2)),
        dma((n,)), dma((n,)),
        dma((n,)), dma((n,)),
    ]
    return pl.pallas_call(
        kernel,
        out_shape=jax.ShapeDtypeStruct((OUT_ROWS, OCC * SUB), bf),
        in_specs=[vmem, vmem, vmem, pl.BlockSpec(memory_space=pl.ANY)],
        out_specs=vmem,
        scratch_shapes=scratch,
        compiler_params=pltpu.CompilerParams(
            collective_id=0, has_side_effects=True, vmem_limit_bytes=58 * 2**20
        ),
        name="ladder",
    )(amps, ab_irrep.reshape(1024, 1), cd_irrep.reshape(1, DEPTH), integrals)


def solution(mesh):
    in_specs = (P("row", "depth"), P("depth", "row", "col"), P("row"), P("depth"))
    out_specs = P(("row", "depth"), "col")
    return jax.shard_map(local, mesh=mesh, in_specs=in_specs, out_specs=out_specs, check_vma=False)
```

time: 304 us -> 95.2 us (0.31)
  waiting for transfers between devices: 212 us -> 0 us
  Pallas kernels: 0 us -> 88.1 us
  blocking collectives: 41.8 us -> 0 us
  between operations: 13.4 us -> 0.02 us
  matrix products: 12.8 us -> 0 us
  local copies, waits for them, and re-layouts: 17 us -> 6.86 us
  other arithmetic: 5.42 us -> 0 us
    all_gather x1 -> x0, waiting for transfers between devices: 118 us -> none  [local(): lax.all_gather(amplitudes, 'row', axis=1, tiled=True)]
    reduce_scatter x1 -> x0, waiting for transfers between devices: 94.7 us -> none  [local(): ladder = lax.psum_scatter(total, 'depth', scatter_dimension=0, tiled=True)]
    pallas_call x0 -> x1, Pallas kernels: none -> 88.1 us  [local(): pl.pallas_call(kernel, out_shape=jax.ShapeDtypeStruct((OUT_ROWS, OCC * SU...]
    all_to_all x1 -> x0, blocking collectives: 41.8 us -> none  [local(): lax.all_to_all(cube, 'col', split_axis=2, concat_axis=1, tiled=True)]
    dot_general x1 -> x0, matrix products: 12.8 us -> none  [local(): jnp.einsum('rck,ckj->rj', shaped, lax.all_gather(amplitudes, 'row', axis=...]
    all_to_all x2 -> x0, local copies, waits for them, and re-layouts: 6.28 us -> none  [local(): lax.all_to_all(cube, 'col', split_axis=2, concat_axis=1, tiled=True)]
    unnamed x6 -> x2, local copies, waits for them, and re-layouts: 4.81 us -> 0.01 us
    convert_element_type x1 -> x0, other arithmetic: 3.24 us -> none  [local(): return result.reshape(out_rows, columns).astype(jnp.bfloat16)]
  transfers between devices with their start and end apart: 2 -> 0, of which waited for: 2 -> 0; matrix products, arithmetic and copies ran while one was open for 2% -> 0% of each run, Pallas kernels for 0% -> 0%
where the time goes in v1:
time: 95.2 us; the launch traced here: 95 us
  Pallas kernels  88.1 us (93%)
  local copies, waits for them, and re-layouts  6.86 us (7%)
    pallas_call x1, Pallas kernels, local(): pl.pallas_call(kernel, out_shape=jax.ShapeDtypeStruct((OUT_ROWS, OCC * SU...  88.1 us
    pallas_call x1, local copies, waits for them, and re-layouts, local(): pl.pallas_call(kernel, out_shape=jax.ShapeDtypeStruct((OUT_ROWS, OCC * SU...  2.45 us

profile of v1, /device:TPU:1, one launch (start us, length us, event | category | flops | bytes accessed | tf_op | source)
XLA Modules:
  0.0 95.0 jit_solution(2942140965033490664)
XLA Ops:
  0.0 0.0 copy-start
  0.0 1.3 %reshape.11.cd_ref = s32[1,1280]{1,0:T(1,128)} reshape(s32[1280]{0:T(1024)} %param.7) | data formatting | bytes 10240 | tf_op jit(solution)/shard_map/reshape | solution.py:384
  1.3 1.3 %reshape.9 = bf16[80,2500]{1,0:T(8,128)(2,1)S(1)} reshape(bf16[40,2,2500]{2,1,0:T(2,128)(2,1)} %param.5) | data formatting | bytes 800000 | tf_op jit(solution)/shard_map/reshape | solution.py:338
  2.6 0.8 pad.4.t_ref
  3.4 0.0 copy-done
  3.4 1.0 %copy.6.ab_ref = s32[1024,1]{1,0:T(8,128)} copy(s32[1024,1]{0,1:T(1,128)S(1)} %bitcast.1) | data formatting | bytes 8192 | tf_op jit(solution)/shard_map/reshape | solution.py:384
  4.4 88.1 %ladder.1 = bf16[256,2500]{1,0:T(8,128)(2,1)} custom-call(bf16[80,2560]{1,0:T(8,128)(2,1)} %pad.4.t_ref, s32[1024,1]{1,0:T(8,128)} %copy.6.ab_ref, s32[1,1280]{1,0:T(1,128)} %reshape.11.cd_ref, bf16[1024,1280]{1,0:T(8,128)(2,1)} %v_hbm.1), custom_call_target="tpu_custom_call" | custom-call | tf_op jit(solution)/shard_map/ladder/pallas_call | solution.py:374
  92.5 2.4 %copy.7 = bf16[256,2500]{0,1:T(8,128)(2,1)} copy(bf16[256,2500]{1,0:T(8,128)(2,1)} %ladder.1) | data formatting | bytes 2560000 | tf_op jit(solution)/shard_map/ladder/pallas_call | solution.py:374
Async XLA Ops:
  0.0 3.4 %copy-start = (s32[1024]{0:T(1024)S(1)}, s32[1024]{0:T(1024)}, u32[]{:S(2)}) copy-start(s32[1024]{0:T(1024)} %param.6) | copy-start | bytes 12292

commit v2 on v1

--- a/solution.py
+++ b/solution.py
@@ -52,9 +52,9 @@
 
 
 def kernel(
-    t_ref, ab_ref, cd_ref, v_hbm, out_ref,
-    v_ref, vp_ref, pk_ref, pt_ref, x_ref, wsend, wrecv, bq, sc_ref, bhl,
-    csend, crecv, ysend, yrecv, own, r_own, r_recv, g_ref, src_ref, sgn_ref, acc_ref,
+    amp_ref, ab_ref, cd_ref, v_hbm, out_ref,
+    t_ref, v_ref, vp_ref, pk_ref, pt_ref, x_ref, wsend, wrecv, bq, sc_ref, bhl,
+    csend, crecv, ysend, ycode, yrecv, own, r_own, r_recv, g_ref, src_ref, sgn_ref, acc_ref,
     v_sem, w_ss, w_rs, h_ss, h_rs, zr_ss, zr_rs, zl_ss, zl_rs, c_ss, c_rs, y_ss, y_rs, m_ss, m_rs,
 ):
     row, c, depth = lax.axis_index("row"), lax.axis_index("col"), lax.axis_index("depth")
@@ -81,6 +81,9 @@
     for dev in (d_right, d_left, d_hi, d_core, d_lo, x_next, x_opp, x_prev):
         pl.semaphore_signal(barrier, inc=1, device_id=dev, device_id_type=MESH)
 
+    t_ref[:, 2432:] = jnp.zeros((ROWS_T, LANES), jnp.bfloat16)
+    t_ref[:, : OCC * SUB] = amp_ref[...]
+
     u = iota((1, HALF), 1) - PAD
     a = div25(u)
     b = u - SUB * a
@@ -130,12 +133,13 @@
     def make_vp(i, _):
         base = pl.multiple_of(i * 128, 128)
         rows = pl.ds(base, 128)
-        keep = ab_ref[rows, :] == cd_ref[...]
+        label = jnp.broadcast_to(ab_ref[rows].reshape(1, 128), (128, 128)).T
+        keep = jnp.concatenate([label] * 10, axis=1) == cd_ref[...].reshape(1, DEPTH)
         masked = jnp.where(keep, v_ref[rows, :].astype(jnp.float32), 0.0).astype(jnp.bfloat16)
         vp_ref[rows, :] = dot(masked, pk_ref[...]).astype(jnp.bfloat16)
         return 0
 
-    lax.fori_loop(0, 8, make_vp, 0)
+    lax.fori_loop(0, 4, make_vp, 0)
 
     w0.wait_recv()
     w1.wait_recv()
@@ -161,6 +165,15 @@
     def hi_copy(n):
         return copy(bq.at[n, z, yh], bq.at[n, z, yh], h_ss.at[n], h_rs.at[n], d_hi)
 
+    def first_copies(n, side):
+        at = yh if side == 0 else 1 - yh
+        ref = bq.at[n, z, at]
+        sem = 4 * side
+        return (
+            copy(ref, ref, zr_ss.at[n, sem], zr_rs.at[n, sem], d_right),
+            copy(ref, ref, zl_ss.at[n, sem], zl_rs.at[n, sem], d_left),
+        )
+
     def right_copy(n, s):
         at = (z - s + NZ) % NZ
         return copy(bq.at[n, at], bq.at[n, at], zr_ss.at[n, s], zr_rs.at[n, s], d_right)
@@ -181,14 +194,23 @@
         return copy(csend.at[n, h], crecv.at[n, h], c_ss.at[n, h], c_rs.at[n, h], d_core)
 
     def lo_copy(n):
-        return copy(ysend.at[n], yrecv.at[n], y_ss.at[n], y_rs.at[n], d_lo)
+        return copy(ycode.at[n], yrecv.at[n], y_ss.at[n], y_rs.at[n], d_lo)
 
     def mirror_copy(n):
         to = (row, (c + 2 - n // 5) % 4, depth)
         return copy(r_own.at[n], r_recv.at[n], m_ss.at[n], m_rs.at[n], to)
 
-    hi_copy(0).start()
-    hi_copy(1).start()
+    def start_both(pair):
+        for one in pair:
+            one.start()
+
+    def own_start(n, _):
+        hi_copy(n).start()
+        start_both(first_copies(n, 0))
+        return 0
+
+    lax.fori_loop(0, CHUNKS, own_start, 0)
+    lax.fori_loop(4, 8, make_vp, 0)
 
     lane = iota((1, WIDE), 1)
     a = div100(lane)
@@ -217,102 +239,154 @@
         both = dot(vp_ref[pl.ds(at, OUT_ROWS), :], bhl[...])
         return both[:, :LANES] + both[:, LANES:]
 
-    def step(t, _):
-        n4 = t - 3
-
-        @pl.when((n4 >= 0) & (n4 < CHUNKS))
-        def _():
-            right_copy(n4, 2).wait_recv()
-            right_last(n4).start()
-            left_copy(n4, 2).wait_recv()
-            left_last(n4).start()
-
-        n3 = t - 2
-
-        @pl.when((n3 >= 0) & (n3 < CHUNKS))
-        def _():
-            right_copy(n3, 1).wait_recv()
-            right_copy(n3, 2).start()
-            left_copy(n3, 1).wait_recv()
-            left_copy(n3, 2).start()
-
-        n2 = t - 1
-
-        @pl.when((n2 >= 0) & (n2 < CHUNKS))
-        def _():
-            right_copy(n2, 0).wait_recv()
-            right_copy(n2, 1).start()
-            left_copy(n2, 0).wait_recv()
-            left_copy(n2, 1).start()
-
-        @pl.when(t + 2 < CHUNKS)
-        def _():
-            hi_copy(t + 2).start()
-
-        @pl.when(t < CHUNKS)
-        def _():
-            hi_copy(t).wait_recv()
-            right_copy(t, 0).start()
-            left_copy(t, 0).start()
-
-        n = t - 4
-
-        @pl.when((n >= 0) & (n < CHUNKS))
-        def _():
-            right_last(n).wait_recv()
-            left_last(n).wait_recv()
-            q = bq[n].reshape(DEPTH, LANES).astype(jnp.int32)
-
-            @pl.when(n == 0)
+    def part_start(n):
+        hi_copy(n).wait_recv()
+        start_both(first_copies(n, 1))
+
+    def forward(n, s):
+        before = [(right_copy(n, s - 1), left_copy(n, s - 1))] if s > 1 else [first_copies(n, 0), first_copies(n, 1)]
+        after = (right_last(n), left_last(n)) if s == 3 else (right_copy(n, s), left_copy(n, s))
+        for side in range(2):
+            for pair in before:
+                pair[side].wait_recv()
+            after[side].start()
+
+    def make_g(n):
+        r = iota((2 * LANES, 512), 0)
+        r = r + (n * LANES + jnp.where(r >= LANES, 2048 - LANES, 0))
+        for w in range(WIDE // 512):
+            at = slice(w * 512, (w + 1) * 512)
+            g_ref[n, :, at] = jnp.where(r == src_ref[:, at], sgn_ref[:, at], 0.0).astype(jnp.bfloat16)
+
+    def expand(n):
+        right_last(n).wait_recv()
+        left_last(n).wait_recv()
+        q = bq[n].reshape(DEPTH, LANES).astype(jnp.int32)
+
+        @pl.when(n == 0)
+        def _():
+            sc_ref[...] = jnp.broadcast_to(jnp.exp2(q[:, 0:1].astype(jnp.float32)), (DEPTH, LANES))
+
+        s = sc_ref[...]
+        hi = (q + 128) >> 8
+        lo = q - (hi << 8)
+        bhl[:, :LANES] = (hi.astype(jnp.float32) * (s * 256.0)).astype(jnp.bfloat16)
+        bhl[:, LANES:] = (lo.astype(jnp.float32) * s).astype(jnp.bfloat16)
+
+    def to_core(n, h):
+        csend[n, h] = block(yl if h else 1 - yl, 1 - core)
+        core_copy(n, h).start()
+
+    def core_sum(n):
+        core_copy(n, 0).wait_recv()
+        part = ysend[n] + crecv[n, 0]
+        biggest = jnp.max(jnp.abs(part), axis=1, keepdims=True)
+        ex = jnp.ceil(jnp.log2(jnp.maximum(biggest, 1e-30))) - 15.0
+        ex = jnp.broadcast_to(ex, (OUT_ROWS, LANES))
+        q = jnp.clip(jnp.floor(part * jnp.exp2(-ex) + 0.5), -32767.0, 32767.0)
+        ycode[n, :OUT_ROWS] = q.astype(jnp.int32).astype(jnp.int16)
+        turned = jnp.concatenate([ex[:LANES].T[:8], ex[LANES:].T[:8]], axis=0)
+        ycode[n, OUT_ROWS:] = turned.astype(jnp.int32).astype(jnp.int16)
+        lo_copy(n).start()
+        core_copy(n, 1).wait_recv()
+        own[n] += crecv[n, 1]
+
+    def finish(n):
+        lo_copy(n).wait_recv()
+        ex = yrecv[n, OUT_ROWS:].astype(jnp.int32).astype(jnp.float32)
+        for k in range(2):
+            rows = slice(k * LANES, (k + 1) * LANES)
+            scale = jnp.exp2(jnp.broadcast_to(ex[8 * k:8 * k + 1], (LANES, LANES)).T)
+            got = yrecv[n, rows].astype(jnp.int32).astype(jnp.float32) * scale
+            r_own[n, rows] = (own[n, rows] + got).astype(jnp.bfloat16)
+        mirror_copy(n).start()
+
+    def place(n):
+        mirror_copy(n).wait_recv()
+        both = jnp.concatenate([r_own[n], r_recv[n]], axis=1)
+        for w in range(WIDE // 512):
+            at = slice(w * 512, (w + 1) * 512)
+            acc_ref[:, at] += dot(both, g_ref[n, :, at])
+
+    def first_part(n, _):
+        part_start(n)
+        return 0
+
+    lax.fori_loop(0, 5, first_part, 0)
+
+    def early(n, _):
+        forward(n, 1)
+        make_g(n)
+        return 0
+
+    def middle(n, _):
+        forward(n, 2)
+        make_g(n + 5)
+        return 0
+
+    def late(n, _):
+        forward(n, 3)
+        part_start(n + 5)
+        return 0
+
+    lax.fori_loop(0, 5, early, 0)
+    lax.fori_loop(0, 5, middle, 0)
+    lax.fori_loop(0, 5, late, 0)
+
+    def event(i):
+        n = 5 + i % 5
+        for s in range(1, 4):
+
+            @pl.when(i // 5 == s - 1)
             def _():
-                sc_ref[...] = jnp.broadcast_to(jnp.exp2(q[:, 0:1].astype(jnp.float32)), (DEPTH, LANES))
-
-            s = sc_ref[...]
-            hi = (q + 128) >> 8
-            lo = q - (hi << 8)
-            bhl[:, :LANES] = (hi.astype(jnp.float32) * (s * 256.0)).astype(jnp.bfloat16)
-            bhl[:, LANES:] = (lo.astype(jnp.float32) * s).astype(jnp.bfloat16)
-            csend[n, 0] = block(1 - yl, 1 - core)
-            core_copy(n, 0).start()
-            csend[n, 1] = block(yl, 1 - core)
-            core_copy(n, 1).start()
-            part = block(1 - yl, core)
-            core_copy(n, 0).wait_recv()
-            ysend[n] = part + crecv[n, 0]
-            lo_copy(n).start()
-            part = block(yl, core)
-            core_copy(n, 1).wait_recv()
-            own[n] = part + crecv[n, 1]
-
-        f = t - 5
-
-        @pl.when((f >= 0) & (f < CHUNKS))
-        def _():
-            lo_copy(f).wait_recv()
-            r_own[f] = (own[f] + yrecv[f]).astype(jnp.bfloat16)
-            mirror_copy(f).start()
-
-        @pl.when(t < CHUNKS)
-        def _():
-            r = iota((2 * LANES, 512), 0)
-            r = r + (t * LANES + jnp.where(r >= LANES, 2048 - LANES, 0))
-            for w in range(WIDE // 512):
-                at = slice(w * 512, (w + 1) * 512)
-                g_ref[t, :, at] = jnp.where(r == src_ref[:, at], sgn_ref[:, at], 0.0).astype(jnp.bfloat16)
-
-        h = t - 6
-
-        @pl.when((h >= 0) & (h < CHUNKS))
-        def _():
-            mirror_copy(h).wait_recv()
-            both = jnp.concatenate([r_own[h], r_recv[h]], axis=1)
-            for w in range(WIDE // 512):
-                at = slice(w * 512, (w + 1) * 512)
-                acc_ref[:, at] += dot(both, g_ref[h, :, at])
-
-        return 0
-
-    lax.fori_loop(0, CHUNKS + 6, step, 0)
+                forward(n, s)
+
+    def body(t, _):
+        @pl.when(t < 5)
+        def _():
+            event(3 * t)
+
+        expand(t)
+        to_core(t, 0)
+        to_core(t, 1)
+
+        @pl.when(t < 5)
+        def _():
+            event(3 * t + 1)
+
+        @pl.when(t >= 1)
+        def _():
+            core_sum(t - 1)
+
+        ysend[t] = block(1 - yl, core)
+        own[t] = block(yl, core)
+
+        @pl.when(t < 5)
+        def _():
+            event(3 * t + 2)
+
+        @pl.when(t >= 3)
+        def _():
+            finish(t - 3)
+
+        return 0
+
+    lax.fori_loop(0, CHUNKS, body, 0)
+
+    def place_some(n, _):
+        place(n)
+        return 0
+
+    def finish_some(n, _):
+        finish(n)
+        return 0
+
+    lax.fori_loop(0, 3, place_some, 0)
+    core_sum(9)
+    lax.fori_loop(7, 9, finish_some, 0)
+    lax.fori_loop(3, 6, place_some, 0)
+    finish(9)
+    lax.fori_loop(6, 10, place_some, 0)
     out_ref[...] = acc_ref[:, : OCC * SUB].astype(jnp.bfloat16)
 
     w0.wait_send()
@@ -320,7 +394,10 @@
 
     def drain(n, _):
         hi_copy(n).wait_send()
-        for s in range(3):
+        for side in range(2):
+            for one in first_copies(n, side):
+                one.wait_send()
+        for s in range(1, 3):
             right_copy(n, s).wait_send()
             left_copy(n, s).wait_send()
         right_last(n).wait_send()
@@ -335,12 +412,13 @@
 
 
 def local(integrals, amplitudes, ab_irrep, cd_irrep):
-    amps = jnp.pad(amplitudes.reshape(ROWS_T, OCC * SUB), ((0, 0), (0, WIDE - OCC * SUB)))
+    amps = amplitudes.reshape(ROWS_T, OCC * SUB)
     vmem = pl.BlockSpec(memory_space=pltpu.VMEM)
     bf, f32 = jnp.bfloat16, jnp.float32
     dma = pltpu.SemaphoreType.DMA
     n = CHUNKS
     scratch = [
+        pltpu.VMEM((ROWS_T, WIDE), bf),
         pltpu.VMEM((1024, DEPTH), bf),
         pltpu.VMEM((1024, DEPTH), bf),
         pltpu.VMEM((DEPTH, DEPTH), bf),
@@ -354,7 +432,8 @@
         pltpu.VMEM((n, 2, OUT_ROWS, LANES), f32),
         pltpu.VMEM((n, 2, OUT_ROWS, LANES), f32),
         pltpu.VMEM((n, OUT_ROWS, LANES), f32),
-        pltpu.VMEM((n, OUT_ROWS, LANES), f32),
+        pltpu.VMEM((n, OUT_ROWS + 16, LANES), jnp.int16),
+        pltpu.VMEM((n, OUT_ROWS + 16, LANES), jnp.int16),
         pltpu.VMEM((n, OUT_ROWS, LANES), f32),
         pltpu.VMEM((n, OUT_ROWS, LANES), bf),
         pltpu.VMEM((n, OUT_ROWS, LANES), bf),
@@ -365,8 +444,8 @@
         dma,
         dma((2,)), dma((2,)),
         dma((n,)), dma((n,)),
-        dma((n, 4)), dma((n, 4)),
-        dma((n, 4)), dma((n, 4)),
+        dma((n, 5)), dma((n, 5)),
+        dma((n, 5)), dma((n, 5)),
         dma((n, 2)), dma((n, 2)),
         dma((n,)), dma((n,)),
         dma((n,)), dma((n,)),
@@ -381,7 +460,7 @@
             collective_id=0, has_side_effects=True, vmem_limit_bytes=58 * 2**20
         ),
         name="ladder",
-    )(amps, ab_irrep.reshape(1024, 1), cd_irrep.reshape(1, DEPTH), integrals)
+    )(amps, ab_irrep, cd_irrep, integrals)
 
 
 def solution(mesh):

time: 95.2 us -> 75.6 us (0.79)
  Pallas kernels: 88.1 us -> 70.6 us
  local copies, waits for them, and re-layouts: 6.86 us -> 4.47 us
    pallas_call x1, Pallas kernels: 88.1 us -> 70.6 us  [local(): pl.pallas_call(kernel, out_shape=jax.ShapeDtypeStruct((OUT_ROWS, OCC * SU...]
    reshape x3 -> x1, local copies, waits for them, and re-layouts: 3.61 us -> 2.03 us  [local(): amps = amplitudes.reshape(ROWS_T, OCC * SUB)]
where the time goes in v2:
time: 75.6 us; the launch traced here: 75.1 us
  Pallas kernels  70.6 us (93%)
  local copies, waits for them, and re-layouts  4.47 us (6%)
    pallas_call x1, Pallas kernels, local(): pl.pallas_call(kernel, out_shape=jax.ShapeDtypeStruct((OUT_ROWS, OCC * SU...  70.6 us
    pallas_call x1, local copies, waits for them, and re-layouts, local(): pl.pallas_call(kernel, out_shape=jax.ShapeDtypeStruct((OUT_ROWS, OCC * SU...  2.45 us
    reshape x1, local copies, waits for them, and re-layouts, local(): amps = amplitudes.reshape(ROWS_T, OCC * SUB)  2.03 us

profile of v2, /device:TPU:1, one launch (start us, length us, event | category | flops | bytes accessed | tf_op | source)
XLA Modules:
  0.0 75.1 jit_solution(3738104154437599700)
XLA Ops:
  0.0 2.0 %reshape.3.amp_ref = bf16[80,2500]{1,0:T(8,128)(2,1)} reshape(bf16[40,2,2500]{2,1,0:T(2,128)(2,1)} %param.5) | data formatting | bytes 800000 | tf_op jit(solution)/shard_map/reshape | solution.py:415
  2.0 70.6 %ladder.1 = bf16[256,2500]{1,0:T(8,128)(2,1)} custom-call(bf16[80,2500]{1,0:T(8,128)(2,1)} %reshape.3.amp_ref, s32[1024]{0:T(1024)} %ab_ref.1, s32[1280]{0:T(1024)} %cd_ref.1, bf16[1024,1280]{1,0:T(8,128)(2,1)} %v_hbm.1), custom_call_target="tpu_custom_call" | custom-call | tf_op jit(solution)/shard_map/ladder/pallas_call | solution.py:453
  72.7 2.4 %copy.5 = bf16[256,2500]{0,1:T(8,128)(2,1)} copy(bf16[256,2500]{1,0:T(8,128)(2,1)} %ladder.1) | data formatting | bytes 2560000 | tf_op jit(solution)/shard_map/ladder/pallas_call | solution.py:453

commit v3 on v2

--- a/solution.py
+++ b/solution.py
@@ -14,7 +14,8 @@
 CHUNKS = 10
 HALF = 640
 PAD = 15
-PAIRS = CHUNKS * LANES
+FIRST = 6
+LAST = CHUNKS - FIRST
 ROWS_T = 80
 DEPTH = 1280
 OUT_ROWS = 256
@@ -82,7 +83,7 @@
         pl.semaphore_signal(barrier, inc=1, device_id=dev, device_id_type=MESH)
 
     t_ref[:, 2432:] = jnp.zeros((ROWS_T, LANES), jnp.bfloat16)
-    t_ref[:, : OCC * SUB] = amp_ref[...]
+    t_ref[:, : OCC * SUB] = amp_ref[...].reshape(ROWS_T, OCC * SUB)
 
     u = iota((1, HALF), 1) - PAD
     a = div25(u)
@@ -212,7 +213,7 @@
     lax.fori_loop(0, CHUNKS, own_start, 0)
     lax.fori_loop(4, 8, make_vp, 0)
 
-    lane = iota((1, WIDE), 1)
+    lane = iota((WIDE, LANES), 0)
     a = div100(lane)
     j = lane - OCC * a
     grp = div25(j)
@@ -252,11 +253,12 @@
             after[side].start()
 
     def make_g(n):
-        r = iota((2 * LANES, 512), 0)
-        r = r + (n * LANES + jnp.where(r >= LANES, 2048 - LANES, 0))
+        col = iota((512, LANES), 1) + n * LANES
         for w in range(WIDE // 512):
             at = slice(w * 512, (w + 1) * 512)
-            g_ref[n, :, at] = jnp.where(r == src_ref[:, at], sgn_ref[:, at], 0.0).astype(jnp.bfloat16)
+            for side in range(2):
+                hit = src_ref[at] == col + 2048 * side
+                g_ref[n, at, side * LANES:(side + 1) * LANES] = jnp.where(hit, sgn_ref[at], 0.0).astype(jnp.bfloat16)
 
     def expand(n):
         right_last(n).wait_recv()
@@ -306,13 +308,15 @@
         both = jnp.concatenate([r_own[n], r_recv[n]], axis=1)
         for w in range(WIDE // 512):
             at = slice(w * 512, (w + 1) * 512)
-            acc_ref[:, at] += dot(both, g_ref[n, :, at])
+            acc_ref[at] += lax.dot_general(
+                g_ref[n, at], both, (((1,), (1,)), ((), ())), preferred_element_type=jnp.float32
+            )
 
     def first_part(n, _):
         part_start(n)
         return 0
 
-    lax.fori_loop(0, 5, first_part, 0)
+    lax.fori_loop(0, FIRST, first_part, 0)
 
     def early(n, _):
         forward(n, 1)
@@ -321,39 +325,43 @@
 
     def middle(n, _):
         forward(n, 2)
-        make_g(n + 5)
+
+        @pl.when(n < LAST)
+        def _():
+            make_g(n + FIRST)
+
         return 0
 
     def late(n, _):
         forward(n, 3)
-        part_start(n + 5)
-        return 0
-
-    lax.fori_loop(0, 5, early, 0)
-    lax.fori_loop(0, 5, middle, 0)
-    lax.fori_loop(0, 5, late, 0)
+
+        @pl.when(n < LAST)
+        def _():
+            part_start(n + FIRST)
+
+        return 0
+
+    lax.fori_loop(0, FIRST, early, 0)
+    lax.fori_loop(0, FIRST, middle, 0)
+    lax.fori_loop(0, FIRST, late, 0)
 
     def event(i):
-        n = 5 + i % 5
+        n = FIRST + i % LAST
         for s in range(1, 4):
 
-            @pl.when(i // 5 == s - 1)
+            @pl.when(i // LAST == s - 1)
             def _():
                 forward(n, s)
 
     def body(t, _):
-        @pl.when(t < 5)
-        def _():
-            event(3 * t)
+        @pl.when(t < FIRST)
+        def _():
+            event(2 * t)
 
         expand(t)
         to_core(t, 0)
         to_core(t, 1)
 
-        @pl.when(t < 5)
-        def _():
-            event(3 * t + 1)
-
         @pl.when(t >= 1)
         def _():
             core_sum(t - 1)
@@ -361,9 +369,9 @@
         ysend[t] = block(1 - yl, core)
         own[t] = block(yl, core)
 
-        @pl.when(t < 5)
-        def _():
-            event(3 * t + 2)
+        @pl.when(t < FIRST)
+        def _():
+            event(2 * t + 1)
 
         @pl.when(t >= 3)
         def _():
@@ -387,7 +395,7 @@
     lax.fori_loop(3, 6, place_some, 0)
     finish(9)
     lax.fori_loop(6, 10, place_some, 0)
-    out_ref[...] = acc_ref[:, : OCC * SUB].astype(jnp.bfloat16)
+    out_ref[...] = acc_ref[: OCC * SUB].astype(jnp.bfloat16)
 
     w0.wait_send()
     w1.wait_send()
@@ -412,7 +420,6 @@
 
 
 def local(integrals, amplitudes, ab_irrep, cd_irrep):
-    amps = amplitudes.reshape(ROWS_T, OCC * SUB)
     vmem = pl.BlockSpec(memory_space=pltpu.VMEM)
     bf, f32 = jnp.bfloat16, jnp.float32
     dma = pltpu.SemaphoreType.DMA
@@ -437,10 +444,10 @@
         pltpu.VMEM((n, OUT_ROWS, LANES), f32),
         pltpu.VMEM((n, OUT_ROWS, LANES), bf),
         pltpu.VMEM((n, OUT_ROWS, LANES), bf),
-        pltpu.VMEM((n, 2 * LANES, WIDE), bf),
-        pltpu.VMEM((1, WIDE), jnp.int32),
-        pltpu.VMEM((1, WIDE), f32),
-        pltpu.VMEM((OUT_ROWS, WIDE), f32),
+        pltpu.VMEM((n, WIDE, 2 * LANES), bf),
+        pltpu.VMEM((WIDE, LANES), jnp.int32),
+        pltpu.VMEM((WIDE, LANES), f32),
+        pltpu.VMEM((WIDE, OUT_ROWS), f32),
         dma,
         dma((2,)), dma((2,)),
         dma((n,)), dma((n,)),
@@ -450,9 +457,9 @@
         dma((n,)), dma((n,)),
         dma((n,)), dma((n,)),
     ]
-    return pl.pallas_call(
+    turned = pl.pallas_call(
         kernel,
-        out_shape=jax.ShapeDtypeStruct((OUT_ROWS, OCC * SUB), bf),
+        out_shape=jax.ShapeDtypeStruct((OCC * SUB, OUT_ROWS), bf),
         in_specs=[vmem, vmem, vmem, pl.BlockSpec(memory_space=pl.ANY)],
         out_specs=vmem,
         scratch_shapes=scratch,
@@ -460,7 +467,8 @@
             collective_id=0, has_side_effects=True, vmem_limit_bytes=58 * 2**20
         ),
         name="ladder",
-    )(amps, ab_irrep, cd_irrep, integrals)
+    )(amplitudes, ab_irrep, cd_irrep, integrals)
+    return turned.T
 
 
 def solution(mesh):

time: 75.6 us -> 74.8 us (0.989)
  local copies, waits for them, and re-layouts: 4.47 us -> 2.44 us
  Pallas kernels: 70.6 us -> 71.8 us
    pallas_call x1 -> x0, local copies, waits for them, and re-layouts: 2.45 us -> none  [local(): pl.pallas_call(kernel, out_shape=jax.ShapeDtypeStruct((OUT_ROWS, OCC * SU...]
    unnamed x0 -> x1, local copies, waits for them, and re-layouts: none -> 2.44 us
    reshape x1 -> x0, local copies, waits for them, and re-layouts: 2.03 us -> none  [local(): amps = amplitudes.reshape(ROWS_T, OCC * SUB)]
    pallas_call x1, Pallas kernels: 70.6 us -> 71.8 us  [local(): pl.pallas_call(kernel, out_shape=jax.ShapeDtypeStruct((OCC * SUB, OUT_ROW...]
where the time goes in v3:
time: 74.8 us; the launch traced here: 74.3 us
  Pallas kernels  71.8 us (96%)
  local copies, waits for them, and re-layouts  2.44 us (3%)
    pallas_call x1, Pallas kernels, local(): pl.pallas_call(kernel, out_shape=jax.ShapeDtypeStruct((OCC * SUB, OUT_ROW...  71.8 us
    unnamed x1, local copies, waits for them, and re-layouts  2.44 us

profile of v3, /device:TPU:1, one launch (start us, length us, event | category | flops | bytes accessed | tf_op | source)
XLA Modules:
  0.0 74.3 jit_solution(16811088357433247452)
XLA Ops:
  0.0 71.8 %ladder.1 = bf16[2500,256]{1,0:T(8,128)(2,1)} custom-call(bf16[40,2,2500]{2,1,0:T(2,128)(2,1)} %amp_ref.1, s32[1024]{0:T(1024)} %ab_ref.1, s32[1280]{0:T(1024)} %cd_ref.1, bf16[1024,1280]{1,0:T(8,128)(2,1)} %v_hbm.1), custom_call_target="tpu_custom_call" | custom-call | tf_op jit(solution)/shard_map/ladder/pallas_call | solution.py:460
  71.8 2.4 %copy.6 = bf16[256,2500]{0,1:T(8,128)(2,1)} copy(bf16[256,2500]{0,1:T(8,128)(2,1)} %bitcast.1) | data formatting | bytes 2560000

commit v4 on v3

--- a/solution.py
+++ b/solution.py
@@ -16,6 +16,9 @@
 PAD = 15
 FIRST = 6
 LAST = CHUNKS - FIRST
+THIN = 3
+FULL = FIRST - THIN
+CUT = 48
 ROWS_T = 80
 DEPTH = 1280
 OUT_ROWS = 256
@@ -56,7 +59,7 @@
     amp_ref, ab_ref, cd_ref, v_hbm, out_ref,
     t_ref, v_ref, vp_ref, pk_ref, pt_ref, x_ref, wsend, wrecv, bq, sc_ref, bhl,
     csend, crecv, ysend, ycode, yrecv, own, r_own, r_recv, g_ref, src_ref, sgn_ref, acc_ref,
-    v_sem, w_ss, w_rs, h_ss, h_rs, zr_ss, zr_rs, zl_ss, zl_rs, c_ss, c_rs, y_ss, y_rs, m_ss, m_rs,
+    v_sem, w_ss, w_rs, h_ss, h_rs, t_ss, t_rs, zr_ss, zr_rs, zl_ss, zl_rs, c_ss, c_rs, y_ss, y_rs, m_ss, m_rs,
 ):
     row, c, depth = lax.axis_index("row"), lax.axis_index("col"), lax.axis_index("depth")
     z, yh = row // 2, row % 2
@@ -182,6 +185,23 @@
     def left_copy(n, s):
         at = (z + s) % NZ
         return copy(bq.at[n, at], bq.at[n, at], zl_ss.at[n, s], zl_rs.at[n, s], d_left)
+
+    def thin_copies(n, s):
+        near, far = (z - s + NZ) % NZ, (z + s) % NZ
+        right, left = bq.at[n, near, yh], bq.at[n, far, yh]
+        if s == 3:
+            right, left = right.at[pl.ds(0, CUT)], left.at[pl.ds(CUT, ROWS_T - CUT)]
+        return (
+            copy(right, right, zr_ss.at[n, s], zr_rs.at[n, s], d_right),
+            copy(left, left, zl_ss.at[n, s], zl_rs.at[n, s], d_left),
+        )
+
+    def slot_copies(n, s):
+        near, far = bq.at[n, (z - s + NZ) % NZ, yh], bq.at[n, (z + s) % NZ, yh]
+        first = copy(near, near, t_ss.at[n - FULL, s - 1], t_rs.at[n - FULL, s - 1], d_hi)
+        if s == 4:
+            return (first,)
+        return first, copy(far, far, t_ss.at[n - FULL, s + 3], t_rs.at[n - FULL, s + 3], d_hi)
 
     def right_last(n):
         at = (z - 3 + NZ) % NZ
@@ -252,6 +272,19 @@
                 pair[side].wait_recv()
             after[side].start()
 
+    def forward_thin(n, s):
+        before = thin_copies(n, s - 1) if s > 1 else first_copies(n, 0)
+        after = thin_copies(n, s)
+        for side in range(2):
+            before[side].wait_recv()
+            after[side].start()
+        start_both(slot_copies(n, s))
+
+    def end_thin(n):
+        for one in thin_copies(n, 3):
+            one.wait_recv()
+        start_both(slot_copies(n, 4))
+
     def make_g(n):
         col = iota((512, LANES), 1) + n * LANES
         for w in range(WIDE // 512):
@@ -260,9 +293,22 @@
                 hit = src_ref[at] == col + 2048 * side
                 g_ref[n, at, side * LANES:(side + 1) * LANES] = jnp.where(hit, sgn_ref[at], 0.0).astype(jnp.bfloat16)
 
+    def is_thin(n):
+        return (n >= FULL) & (n < FIRST)
+
     def expand(n):
-        right_last(n).wait_recv()
-        left_last(n).wait_recv()
+        @pl.when(is_thin(n))
+        def _():
+            hi_copy(n).wait_recv()
+            for s in range(1, 5):
+                for one in slot_copies(n, s):
+                    one.wait_recv()
+
+        @pl.when(jnp.logical_not(is_thin(n)))
+        def _():
+            right_last(n).wait_recv()
+            left_last(n).wait_recv()
+
         q = bq[n].reshape(DEPTH, LANES).astype(jnp.int32)
 
         @pl.when(n == 0)
@@ -316,34 +362,44 @@
         part_start(n)
         return 0
 
-    lax.fori_loop(0, FIRST, first_part, 0)
+    lax.fori_loop(0, FULL, first_part, 0)
 
     def early(n, _):
         forward(n, 1)
         make_g(n)
         return 0
 
+    def early_thin(n, _):
+        forward_thin(n, 1)
+        make_g(n)
+        return 0
+
     def middle(n, _):
         forward(n, 2)
-
-        @pl.when(n < LAST)
-        def _():
-            make_g(n + FIRST)
-
+        make_g(n + FIRST)
+        return 0
+
+    def middle_thin(n, _):
+        forward_thin(n, 2)
         return 0
 
     def late(n, _):
         forward(n, 3)
-
-        @pl.when(n < LAST)
-        def _():
-            part_start(n + FIRST)
-
-        return 0
-
-    lax.fori_loop(0, FIRST, early, 0)
-    lax.fori_loop(0, FIRST, middle, 0)
-    lax.fori_loop(0, FIRST, late, 0)
+        part_start(n + FIRST)
+        return 0
+
+    def late_thin(n, _):
+        forward_thin(n, 3)
+        return 0
+
+    lax.fori_loop(0, FULL, early, 0)
+    lax.fori_loop(FULL, FIRST, early_thin, 0)
+    lax.fori_loop(0, FULL, middle, 0)
+    lax.fori_loop(FULL, FIRST, middle_thin, 0)
+    lax.fori_loop(0, FULL, late, 0)
+    lax.fori_loop(FULL, FIRST, late_thin, 0)
+    part_start(CHUNKS - 1)
+    make_g(CHUNKS - 1)
 
     def event(i):
         n = FIRST + i % LAST
@@ -373,6 +429,11 @@
         def _():
             event(2 * t + 1)
 
+        @pl.when(t == 0)
+        def _():
+            for n in range(FULL, FIRST):
+                end_thin(n)
+
         @pl.when(t >= 3)
         def _():
             finish(t - 3)
@@ -387,36 +448,62 @@
 
     def finish_some(n, _):
         finish(n)
+        return 0
+
+    def drain(n, _):
+        hi_copy(n).wait_send()
+        for one in first_copies(n, 0):
+            one.wait_send()
+
+        @pl.when(is_thin(n))
+        def _():
+            for s in range(1, 4):
+                for one in thin_copies(n, s):
+                    one.wait_send()
+            for s in range(1, 5):
+                for one in slot_copies(n, s):
+                    one.wait_send()
+
+        @pl.when(jnp.logical_not(is_thin(n)))
+        def _():
+            for one in first_copies(n, 1):
+                one.wait_send()
+            for s in range(1, 3):
+                right_copy(n, s).wait_send()
+                left_copy(n, s).wait_send()
+            right_last(n).wait_send()
+            left_last(n).wait_send()
+
+        return 0
+
+    def drain_sums(n, _):
+        core_copy(n, 0).wait_send()
+        core_copy(n, 1).wait_send()
+        lo_copy(n).wait_send()
+        return 0
+
+    def drain_mirror(n, _):
+        mirror_copy(n).wait_send()
         return 0
 
     lax.fori_loop(0, 3, place_some, 0)
     core_sum(9)
     lax.fori_loop(7, 9, finish_some, 0)
-    lax.fori_loop(3, 6, place_some, 0)
+    lax.fori_loop(0, CHUNKS, drain, 0)
+    lax.fori_loop(3, 5, place_some, 0)
     finish(9)
-    lax.fori_loop(6, 10, place_some, 0)
-    out_ref[...] = acc_ref[: OCC * SUB].astype(jnp.bfloat16)
-
     w0.wait_send()
     w1.wait_send()
-
-    def drain(n, _):
-        hi_copy(n).wait_send()
-        for side in range(2):
-            for one in first_copies(n, side):
-                one.wait_send()
-        for s in range(1, 3):
-            right_copy(n, s).wait_send()
-            left_copy(n, s).wait_send()
-        right_last(n).wait_send()
-        left_last(n).wait_send()
-        core_copy(n, 0).wait_send()
-        core_copy(n, 1).wait_send()
-        lo_copy(n).wait_send()
-        mirror_copy(n).wait_send()
-        return 0
-
-    lax.fori_loop(0, CHUNKS, drain, 0)
+    lax.fori_loop(0, CHUNKS, drain_sums, 0)
+    lax.fori_loop(5, 10, place_some, 0)
+    out_ref[...] = acc_ref[: OCC * SUB].astype(jnp.bfloat16)
+    lax.fori_loop(0, CHUNKS, drain_mirror, 0)
+
+
+def pass_on(src, dst, sem):
+    whole = pltpu.make_async_copy(src, dst, sem)
+    whole.start()
+    whole.wait()
 
 
 def local(integrals, amplitudes, ab_irrep, cd_irrep):
@@ -451,6 +538,7 @@
         dma,
         dma((2,)), dma((2,)),
         dma((n,)), dma((n,)),
+        dma((THIN, 7)), dma((THIN, 7)),
         dma((n, 5)), dma((n, 5)),
         dma((n, 5)), dma((n, 5)),
         dma((n, 2)), dma((n, 2)),
@@ -468,7 +556,16 @@
         ),
         name="ladder",
     )(amplitudes, ab_irrep, cd_irrep, integrals)
-    return turned.T
+    any_space = pl.BlockSpec(memory_space=pl.ANY)
+    final = pl.pallas_call(
+        pass_on,
+        out_shape=jax.ShapeDtypeStruct(turned.shape, turned.dtype),
+        in_specs=[any_space],
+        out_specs=any_space,
+        scratch_shapes=[dma],
+        name="pass_on",
+    )(turned)
+    return final.T
 
 
 def solution(mesh):

time: 74.8 us -> 110 us (1.47)
  Pallas kernels: 71.8 us -> 109 us
  local copies, waits for them, and re-layouts: 2.44 us -> 0 us
    pallas_call x0 -> x1, Pallas kernels: none -> 39.9 us  [local(): pl.pallas_call(pass_on, out_shape=jax.ShapeDtypeStruct(turned.shape, turn...]
    unnamed x1 -> x0, local copies, waits for them, and re-layouts: 2.44 us -> none
    pallas_call x1, Pallas kernels: 71.8 us -> 69.5 us  [local(): pl.pallas_call(kernel, out_shape=jax.ShapeDtypeStruct((OCC * SUB, OUT_ROW...]
where the time goes in v4:
time: 110 us; the launch traced here: 109 us
  Pallas kernels  109 us (99%)
    pallas_call x1, Pallas kernels, local(): pl.pallas_call(kernel, out_shape=jax.ShapeDtypeStruct((OCC * SUB, OUT_ROW...  69.5 us
    pallas_call x1, Pallas kernels, local(): pl.pallas_call(pass_on, out_shape=jax.ShapeDtypeStruct(turned.shape, turn...  39.9 us

profile of v4, /device:TPU:1, one launch (start us, length us, event | category | flops | bytes accessed | tf_op | source)
XLA Modules:
  0.0 109.5 jit_solution(11360145147665569276)
XLA Ops:
  0.0 69.5 %ladder.1.src = bf16[2500,256]{1,0:T(8,128)(2,1)} custom-call(bf16[40,2,2500]{2,1,0:T(2,128)(2,1)} %amp_ref.1, s32[1024]{0:T(1024)} %ab_ref.1, s32[1280]{0:T(1024)} %cd_ref.1, bf16[1024,1280]{1,0:T(8,128)(2,1)} %v_hbm.1), custom_call_target="tpu_custom_call" | custom-call | tf_op jit(solution)/shard_map/ladder/pallas_call | solution.py:548
  69.5 39.9 %pass_on.1 = bf16[2500,256]{1,0:T(8,128)(2,1)} custom-call(bf16[2500,256]{1,0:T(8,128)(2,1)} %ladder.1.src), custom_call_target="tpu_custom_call" | custom-call | tf_op jit(solution)/shard_map/pass_on/pallas_call | solution.py:560

commit v5 on v4

--- a/solution.py
+++ b/solution.py
@@ -34,10 +34,6 @@
     return (v * 5243) >> 17
 
 
-def div100(v):
-    return (v * 5243) >> 19
-
-
 def one_hot(cond):
     return jnp.where(cond, 1.0, 0.0).astype(jnp.bfloat16)
 
@@ -58,7 +54,7 @@
 def kernel(
     amp_ref, ab_ref, cd_ref, v_hbm, out_ref,
     t_ref, v_ref, vp_ref, pk_ref, pt_ref, x_ref, wsend, wrecv, bq, sc_ref, bhl,
-    csend, crecv, ysend, ycode, yrecv, own, r_own, r_recv, g_ref, src_ref, sgn_ref, acc_ref,
+    csend, crecv, ysend, ycode, yrecv, own, r_own, r_recv, tmp_ref, acc_ref,
     v_sem, w_ss, w_rs, h_ss, h_rs, t_ss, t_rs, zr_ss, zr_rs, zl_ss, zl_rs, c_ss, c_rs, y_ss, y_rs, m_ss, m_rs,
 ):
     row, c, depth = lax.axis_index("row"), lax.axis_index("col"), lax.axis_index("depth")
@@ -233,28 +229,6 @@
     lax.fori_loop(0, CHUNKS, own_start, 0)
     lax.fori_loop(4, 8, make_vp, 0)
 
-    lane = iota((WIDE, LANES), 0)
-    a = div100(lane)
-    j = lane - OCC * a
-    grp = div25(j)
-    b = j - SUB * grp
-    rel = (grp - c + 4) % 4
-    direct = PAD + SUB * a + b
-    turned = PAD + SUB * b + a
-    src = jnp.where(
-        rel == 0,
-        jnp.where(b > a, direct, jnp.where(b < a, turned, -1)),
-        jnp.where(
-            rel == 1,
-            HALF + direct,
-            jnp.where(rel == 2, jnp.where(b <= a, direct, 2048 + turned), 2048 + HALF + turned),
-        ),
-    )
-    src_ref[...] = jnp.where(lane < OCC * SUB, src, -1)
-    minus = ((rel == 0) & (b < a)) | ((rel == 2) & (b > a)) | (rel == 3)
-    sgn_ref[...] = jnp.where(minus, -1.0, 1.0)
-    acc_ref[...] = jnp.zeros_like(acc_ref)
-
     def block(yl_at, core_at):
         at = pl.multiple_of((2 * yl_at + core_at) * OUT_ROWS, OUT_ROWS)
         both = dot(vp_ref[pl.ds(at, OUT_ROWS), :], bhl[...])
@@ -285,18 +259,10 @@
             one.wait_recv()
         start_both(slot_copies(n, 4))
 
-    def make_g(n):
-        col = iota((512, LANES), 1) + n * LANES
-        for w in range(WIDE // 512):
-            at = slice(w * 512, (w + 1) * 512)
-            for side in range(2):
-                hit = src_ref[at] == col + 2048 * side
-                g_ref[n, at, side * LANES:(side + 1) * LANES] = jnp.where(hit, sgn_ref[at], 0.0).astype(jnp.bfloat16)
-
     def is_thin(n):
         return (n >= FULL) & (n < FIRST)
 
-    def expand(n):
+    def arrive(n):
         @pl.when(is_thin(n))
         def _():
             hi_copy(n).wait_recv()
@@ -309,6 +275,7 @@
             right_last(n).wait_recv()
             left_last(n).wait_recv()
 
+    def expand(n):
         q = bq[n].reshape(DEPTH, LANES).astype(jnp.int32)
 
         @pl.when(n == 0)
@@ -346,17 +313,41 @@
             rows = slice(k * LANES, (k + 1) * LANES)
             scale = jnp.exp2(jnp.broadcast_to(ex[8 * k:8 * k + 1], (LANES, LANES)).T)
             got = yrecv[n, rows].astype(jnp.int32).astype(jnp.float32) * scale
-            r_own[n, rows] = (own[n, rows] + got).astype(jnp.bfloat16)
+            r_own[n, :, rows] = (own[n, rows] + got).T.astype(jnp.bfloat16)
         mirror_copy(n).start()
 
-    def place(n):
+    def place(block_ref, group):
+        for q in range(4):
+
+            @pl.when((c + group) % 4 == q)
+            def _():
+                for a in range(SUB):
+                    at, to = PAD + SUB * a, OCC * a + SUB * q
+                    acc_ref[to:to + SUB, :] = block_ref[at:at + SUB, :]
+
+    def mirror_wait(n, _):
         mirror_copy(n).wait_recv()
-        both = jnp.concatenate([r_own[n], r_recv[n]], axis=1)
-        for w in range(WIDE // 512):
-            at = slice(w * 512, (w + 1) * 512)
-            acc_ref[at] += lax.dot_general(
-                g_ref[n, at], both, (((1,), (1,)), ((), ())), preferred_element_type=jnp.float32
-            )
+        return 0
+
+    def place_opposite():
+        rows = iota((HALF, 1), 0) - PAD
+        ia = div25(rows)
+        ib = rows - SUB * ia
+        mine = r_own[0:5].reshape(HALF, OUT_ROWS)
+        direct = mine.astype(jnp.float32)
+        turned = dot(pt_ref[...], mine)
+        tmp_ref[...] = jnp.where(ib > ia, direct, jnp.where(ib < ia, -turned, 0.0))
+        place(tmp_ref, 0)
+        tmp_ref[...] = jnp.where(ib <= ia, direct, -dot(pt_ref[...], r_recv[0:5].reshape(HALF, OUT_ROWS)))
+        place(tmp_ref, 2)
+
+    def place_next():
+        tmp_ref[...] = r_own[5:10].reshape(HALF, OUT_ROWS).astype(jnp.float32)
+        place(tmp_ref, 1)
+
+    def place_previous():
+        tmp_ref[...] = -dot(pt_ref[...], r_recv[5:10].reshape(HALF, OUT_ROWS))
+        place(tmp_ref, 3)
 
     def first_part(n, _):
         part_start(n)
@@ -366,17 +357,14 @@
 
     def early(n, _):
         forward(n, 1)
-        make_g(n)
         return 0
 
     def early_thin(n, _):
         forward_thin(n, 1)
-        make_g(n)
         return 0
 
     def middle(n, _):
         forward(n, 2)
-        make_g(n + FIRST)
         return 0
 
     def middle_thin(n, _):
@@ -399,7 +387,6 @@
     lax.fori_loop(0, FULL, late, 0)
     lax.fori_loop(FULL, FIRST, late_thin, 0)
     part_start(CHUNKS - 1)
-    make_g(CHUNKS - 1)
 
     def event(i):
         n = FIRST + i % LAST
@@ -414,6 +401,7 @@
         def _():
             event(2 * t)
 
+        arrive(t)
         expand(t)
         to_core(t, 0)
         to_core(t, 1)
@@ -441,10 +429,6 @@
         return 0
 
     lax.fori_loop(0, CHUNKS, body, 0)
-
-    def place_some(n, _):
-        place(n)
-        return 0
 
     def finish_some(n, _):
         finish(n)
@@ -486,24 +470,24 @@
         mirror_copy(n).wait_send()
         return 0
 
-    lax.fori_loop(0, 3, place_some, 0)
     core_sum(9)
     lax.fori_loop(7, 9, finish_some, 0)
     lax.fori_loop(0, CHUNKS, drain, 0)
-    lax.fori_loop(3, 5, place_some, 0)
+    lax.fori_loop(0, 5, mirror_wait, 0)
+    place_opposite()
     finish(9)
     w0.wait_send()
     w1.wait_send()
     lax.fori_loop(0, CHUNKS, drain_sums, 0)
-    lax.fori_loop(5, 10, place_some, 0)
-    out_ref[...] = acc_ref[: OCC * SUB].astype(jnp.bfloat16)
+    place_next()
+    lax.fori_loop(5, CHUNKS, mirror_wait, 0)
+    place_previous()
+    out_ref[...] = acc_ref[...].astype(jnp.bfloat16)
     lax.fori_loop(0, CHUNKS, drain_mirror, 0)
 
 
-def pass_on(src, dst, sem):
-    whole = pltpu.make_async_copy(src, dst, sem)
-    whole.start()
-    whole.wait()
+def pass_on(src, dst):
+    dst[...] = src[...]
 
 
 def local(integrals, amplitudes, ab_irrep, cd_irrep):
@@ -529,12 +513,10 @@
         pltpu.VMEM((n, OUT_ROWS + 16, LANES), jnp.int16),
         pltpu.VMEM((n, OUT_ROWS + 16, LANES), jnp.int16),
         pltpu.VMEM((n, OUT_ROWS, LANES), f32),
-        pltpu.VMEM((n, OUT_ROWS, LANES), bf),
-        pltpu.VMEM((n, OUT_ROWS, LANES), bf),
-        pltpu.VMEM((n, WIDE, 2 * LANES), bf),
-        pltpu.VMEM((WIDE, LANES), jnp.int32),
-        pltpu.VMEM((WIDE, LANES), f32),
-        pltpu.VMEM((WIDE, OUT_ROWS), f32),
+        pltpu.VMEM((n, LANES, OUT_ROWS), bf),
+        pltpu.VMEM((n, LANES, OUT_ROWS), bf),
+        pltpu.VMEM((HALF, OUT_ROWS), f32),
+        pltpu.VMEM((OCC * SUB, OUT_ROWS), f32),
         dma,
         dma((2,)), dma((2,)),
         dma((n,)), dma((n,)),
@@ -556,13 +538,11 @@
         ),
         name="ladder",
     )(amplitudes, ab_irrep, cd_irrep, integrals)
-    any_space = pl.BlockSpec(memory_space=pl.ANY)
     final = pl.pallas_call(
         pass_on,
         out_shape=jax.ShapeDtypeStruct(turned.shape, turned.dtype),
-        in_specs=[any_space],
-        out_specs=any_space,
-        scratch_shapes=[dma],
+        in_specs=[vmem],
+        out_specs=vmem,
         name="pass_on",
     )(turned)
     return final.T

time: 110 us -> 71.9 us (0.65)
  Pallas kernels: 109 us -> 71.4 us
    pallas_call x1, Pallas kernels: 39.9 us -> 2.44 us  [local(): pl.pallas_call(pass_on, out_shape=jax.ShapeDtypeStruct(turned.shape, turn...]
where the time goes in v5:
time: 71.9 us; the launch traced here: 71.4 us
  Pallas kernels  71.4 us (99%)
    pallas_call x1, Pallas kernels, local(): pl.pallas_call(kernel, out_shape=jax.ShapeDtypeStruct((OCC * SUB, OUT_ROW...  69 us
    pallas_call x1, Pallas kernels, local(): pl.pallas_call(pass_on, out_shape=jax.ShapeDtypeStruct(turned.shape, turn...  2.44 us

profile of v5, /device:TPU:1, one launch (start us, length us, event | category | flops | bytes accessed | tf_op | source)
XLA Modules:
  0.0 71.4 jit_solution(14071000423520808357)
XLA Ops:
  0.0 69.0 %ladder.1.src = bf16[2500,256]{1,0:T(8,128)(2,1)} custom-call(bf16[40,2,2500]{2,1,0:T(2,128)(2,1)} %amp_ref.1, s32[1024]{0:T(1024)} %ab_ref.1, s32[1280]{0:T(1024)} %cd_ref.1, bf16[1024,1280]{1,0:T(8,128)(2,1)} %v_hbm.1), custom_call_target="tpu_custom_call" | custom-call | tf_op jit(solution)/shard_map/ladder/pallas_call | solution.py:530
  69.0 2.4 %pass_on.1 = bf16[2500,256]{1,0:T(8,128)(2,1)} custom-call(bf16[2500,256]{1,0:T(8,128)(2,1)} %ladder.1.src), custom_call_target="tpu_custom_call" | custom-call | tf_op jit(solution)/shard_map/pass_on/pallas_call | solution.py:541

commit v6 on v5

--- a/solution.py
+++ b/solution.py
@@ -53,7 +53,7 @@
 
 def kernel(
     amp_ref, ab_ref, cd_ref, v_hbm, out_ref,
-    t_ref, v_ref, vp_ref, pk_ref, pt_ref, x_ref, wsend, wrecv, bq, sc_ref, bhl,
+    t_ref, v_ref, vp_ref, pk_ref, pt_ref, x_ref, diag_ref, wsend, wrecv, bq, sc_ref, bhl,
     csend, crecv, ysend, ycode, yrecv, own, r_own, r_recv, tmp_ref, acc_ref,
     v_sem, w_ss, w_rs, h_ss, h_rs, t_ss, t_rs, zr_ss, zr_rs, zl_ss, zl_rs, c_ss, c_rs, y_ss, y_rs, m_ss, m_rs,
 ):
@@ -105,15 +105,14 @@
         for g in range(4):
             x_ref[g, :, n * LANES:(n + 1) * LANES] = got[:, g * LANES:(g + 1) * LANES]
 
-    wsend[0] = dot(x_ref[3], pt_ref[...]).astype(jnp.bfloat16)
     wsend[1] = dot(x_ref[2], pt_ref[...]).astype(jnp.bfloat16)
     pl.semaphore_wait(barrier, 8)
     w0 = copy(wsend.at[0], wrecv.at[0], w_ss.at[0], w_rs.at[0], x_prev)
     w1 = copy(wsend.at[1], wrecv.at[1], w_ss.at[1], w_rs.at[1], x_opp)
     w1.start()
-    w0.start()
+    wsend[0] = dot(x_ref[3], pt_ref[...]).astype(jnp.bfloat16)
     x0 = x_ref[0]
-    diag = x0.astype(jnp.float32) - dot(x0, pt_ref[...])
+    diag_ref[...] = x0.astype(jnp.float32) - dot(x0, pt_ref[...])
 
     k = iota((1, DEPTH), 1)
     zz = (k * 3277) >> 19
@@ -128,39 +127,30 @@
         return 0
 
     lax.fori_loop(0, DEPTH // 256, make_pk, 0)
+    w1.wait_send()
+    w0.start()
     v_copy.wait()
 
     def make_vp(i, _):
+        to = 512 * jnp.where(i // 2 % 2 == core, 1, 0) + 256 * jnp.where(i // 4 == yl, 1, 0) + 128 * (i % 2)
         base = pl.multiple_of(i * 128, 128)
         rows = pl.ds(base, 128)
         label = jnp.broadcast_to(ab_ref[rows].reshape(1, 128), (128, 128)).T
         keep = jnp.concatenate([label] * 10, axis=1) == cd_ref[...].reshape(1, DEPTH)
         masked = jnp.where(keep, v_ref[rows, :].astype(jnp.float32), 0.0).astype(jnp.bfloat16)
-        vp_ref[rows, :] = dot(masked, pk_ref[...]).astype(jnp.bfloat16)
-        return 0
-
-    lax.fori_loop(0, 4, make_vp, 0)
-
-    w0.wait_recv()
-    w1.wait_recv()
-    ta1 = x_ref[1].astype(jnp.float32) - wrecv[0].astype(jnp.float32)
-    ta2 = jnp.where(lower, x_ref[2].astype(jnp.float32) - wrecv[1].astype(jnp.float32), diag)
-    biggest = jnp.maximum(
-        jnp.max(jnp.abs(ta1), axis=1, keepdims=True), jnp.max(jnp.abs(ta2), axis=1, keepdims=True)
-    )
-    exponent = jnp.ceil(jnp.log2(jnp.maximum(biggest, 1e-30))) - 15.0
-    scale = jnp.exp2(-exponent)
-
-    def coded(v):
-        return jnp.clip(jnp.floor(v * scale + 0.5), -32767.0, 32767.0)
-
-    q2 = coded(ta2)
-    q1 = coded(ta1)
-    q2 = jnp.where(iota((ROWS_T, HALF), 1) < PAD, jnp.broadcast_to(exponent, (ROWS_T, HALF)), q2)
-    for n in range(CHUNKS):
-        q = q2 if n < 5 else q1
-        part = q[:, (n % 5) * LANES:(n % 5 + 1) * LANES]
-        bq[n, z, yh] = part.astype(jnp.int32).astype(jnp.int16)
+        vp_ref[pl.ds(pl.multiple_of(to, 128), 128), :] = dot(masked, pk_ref[...]).astype(jnp.bfloat16)
+        return 0
+
+    lax.fori_loop(0, 2, make_vp, 0)
+
+    def encode(values, chunk):
+        biggest = jnp.max(jnp.abs(values), axis=1, keepdims=True)
+        exponent = jnp.ceil(jnp.log2(jnp.maximum(biggest, 1e-30))) - 15.0
+        q = jnp.clip(jnp.floor(values * jnp.exp2(-exponent) + 0.5), -32767.0, 32767.0)
+        q = jnp.where(iota((ROWS_T, HALF), 1) < PAD, jnp.broadcast_to(exponent, (ROWS_T, HALF)), q)
+        for n in range(5):
+            part = q[:, n * LANES:(n + 1) * LANES]
+            bq[chunk + n, z, yh] = part.astype(jnp.int32).astype(jnp.int16)
 
     def hi_copy(n):
         return copy(bq.at[n, z, yh], bq.at[n, z, yh], h_ss.at[n], h_rs.at[n], d_hi)
@@ -226,12 +216,18 @@
         start_both(first_copies(n, 0))
         return 0
 
-    lax.fori_loop(0, CHUNKS, own_start, 0)
-    lax.fori_loop(4, 8, make_vp, 0)
-
-    def block(yl_at, core_at):
-        at = pl.multiple_of((2 * yl_at + core_at) * OUT_ROWS, OUT_ROWS)
-        both = dot(vp_ref[pl.ds(at, OUT_ROWS), :], bhl[...])
+    w1.wait_recv()
+    opposite = x_ref[2].astype(jnp.float32) - wrecv[1].astype(jnp.float32)
+    encode(jnp.where(lower, opposite, diag_ref[...]), 0)
+    lax.fori_loop(0, 5, own_start, 0)
+    make_vp(2, 0)
+    w0.wait_recv()
+    encode(x_ref[1].astype(jnp.float32) - wrecv[0].astype(jnp.float32), 5)
+    lax.fori_loop(5, CHUNKS, own_start, 0)
+    make_vp(3, 0)
+
+    def products(half):
+        both = dot(vp_ref[512 * half:512 * half + 512, :], bhl[...])
         return both[:, :LANES] + both[:, LANES:]
 
     def part_start(n):
@@ -278,7 +274,7 @@
     def expand(n):
         q = bq[n].reshape(DEPTH, LANES).astype(jnp.int32)
 
-        @pl.when(n == 0)
+        @pl.when((n == 0) | (n == 5))
         def _():
             sc_ref[...] = jnp.broadcast_to(jnp.exp2(q[:, 0:1].astype(jnp.float32)), (DEPTH, LANES))
 
@@ -288,20 +284,24 @@
         bhl[:, :LANES] = (hi.astype(jnp.float32) * (s * 256.0)).astype(jnp.bfloat16)
         bhl[:, LANES:] = (lo.astype(jnp.float32) * s).astype(jnp.bfloat16)
 
-    def to_core(n, h):
-        csend[n, h] = block(yl if h else 1 - yl, 1 - core)
-        core_copy(n, h).start()
+    def to_core(n):
+        csend[n] = products(0).reshape(2, OUT_ROWS, LANES)
+        core_copy(n, 0).start()
+        core_copy(n, 1).start()
+
+    def keep(n):
+        both = products(1)
+        ysend[n] = both[:OUT_ROWS]
+        own[n] = both[OUT_ROWS:]
 
     def core_sum(n):
         core_copy(n, 0).wait_recv()
         part = ysend[n] + crecv[n, 0]
-        biggest = jnp.max(jnp.abs(part), axis=1, keepdims=True)
+        biggest = jnp.max(jnp.abs(part), axis=0, keepdims=True)
         ex = jnp.ceil(jnp.log2(jnp.maximum(biggest, 1e-30))) - 15.0
-        ex = jnp.broadcast_to(ex, (OUT_ROWS, LANES))
         q = jnp.clip(jnp.floor(part * jnp.exp2(-ex) + 0.5), -32767.0, 32767.0)
         ycode[n, :OUT_ROWS] = q.astype(jnp.int32).astype(jnp.int16)
-        turned = jnp.concatenate([ex[:LANES].T[:8], ex[LANES:].T[:8]], axis=0)
-        ycode[n, OUT_ROWS:] = turned.astype(jnp.int32).astype(jnp.int16)
+        ycode[n, OUT_ROWS:] = jnp.broadcast_to(ex, (16, LANES)).astype(jnp.int32).astype(jnp.int16)
         lo_copy(n).start()
         core_copy(n, 1).wait_recv()
         own[n] += crecv[n, 1]
@@ -309,11 +309,8 @@
     def finish(n):
         lo_copy(n).wait_recv()
         ex = yrecv[n, OUT_ROWS:].astype(jnp.int32).astype(jnp.float32)
-        for k in range(2):
-            rows = slice(k * LANES, (k + 1) * LANES)
-            scale = jnp.exp2(jnp.broadcast_to(ex[8 * k:8 * k + 1], (LANES, LANES)).T)
-            got = yrecv[n, rows].astype(jnp.int32).astype(jnp.float32) * scale
-            r_own[n, :, rows] = (own[n, rows] + got).T.astype(jnp.bfloat16)
+        got = yrecv[n, :OUT_ROWS].astype(jnp.int32).astype(jnp.float32) * jnp.exp2(ex[0:1])
+        r_own[n] = (own[n] + got).T.astype(jnp.bfloat16)
         mirror_copy(n).start()
 
     def place(block_ref, group):
@@ -354,6 +351,7 @@
         return 0
 
     lax.fori_loop(0, FULL, first_part, 0)
+    lax.fori_loop(4, 8, make_vp, 0)
 
     def early(n, _):
         forward(n, 1)
@@ -403,15 +401,13 @@
 
         arrive(t)
         expand(t)
-        to_core(t, 0)
-        to_core(t, 1)
+        to_core(t)
 
         @pl.when(t >= 1)
         def _():
             core_sum(t - 1)
 
-        ysend[t] = block(1 - yl, core)
-        own[t] = block(yl, core)
+        keep(t)
 
         @pl.when(t < FIRST)
         def _():
@@ -477,17 +473,12 @@
     place_opposite()
     finish(9)
     w0.wait_send()
-    w1.wait_send()
     lax.fori_loop(0, CHUNKS, drain_sums, 0)
     place_next()
     lax.fori_loop(5, CHUNKS, mirror_wait, 0)
     place_previous()
     out_ref[...] = acc_ref[...].astype(jnp.bfloat16)
     lax.fori_loop(0, CHUNKS, drain_mirror, 0)
-
-
-def pass_on(src, dst):
-    dst[...] = src[...]
 
 
 def local(integrals, amplitudes, ab_irrep, cd_irrep):
@@ -502,6 +493,7 @@
         pltpu.VMEM((DEPTH, DEPTH), bf),
         pltpu.VMEM((HALF, HALF), bf),
         pltpu.VMEM((4, ROWS_T, HALF), bf),
+        pltpu.VMEM((ROWS_T, HALF), f32),
         pltpu.VMEM((2, ROWS_T, HALF), bf),
         pltpu.VMEM((2, ROWS_T, HALF), bf),
         pltpu.VMEM((n, NZ, 2, ROWS_T, LANES), jnp.int16),
@@ -538,14 +530,7 @@
         ),
         name="ladder",
     )(amplitudes, ab_irrep, cd_irrep, integrals)
-    final = pl.pallas_call(
-        pass_on,
-        out_shape=jax.ShapeDtypeStruct(turned.shape, turned.dtype),
-        in_specs=[vmem],
-        out_specs=vmem,
-        name="pass_on",
-    )(turned)
-    return final.T
+    return turned.T
 
 
 def solution(mesh):

time: 71.9 us -> 70.8 us (0.985)
  Pallas kernels: 71.4 us -> 68.2 us
  local copies, waits for them, and re-layouts: 0 us -> 2.44 us
    pallas_call x1 -> x0, Pallas kernels: 2.44 us -> none  [local(): pl.pallas_call(pass_on, out_shape=jax.ShapeDtypeStruct(turned.shape, turn...]
    unnamed x0 -> x1, local copies, waits for them, and re-layouts: none -> 2.44 us
    pallas_call x1, Pallas kernels: 69 us -> 68.2 us  [local(): pl.pallas_call(kernel, out_shape=jax.ShapeDtypeStruct((OCC * SUB, OUT_ROW...]
where the time goes in v6:
time: 70.8 us; the launch traced here: 70.7 us
  Pallas kernels  68.2 us (96%)
  local copies, waits for them, and re-layouts  2.44 us (3%)
    pallas_call x1, Pallas kernels, local(): pl.pallas_call(kernel, out_shape=jax.ShapeDtypeStruct((OCC * SUB, OUT_ROW...  68.2 us
    unnamed x1, local copies, waits for them, and re-layouts  2.44 us

profile of v6, /device:TPU:1, one launch (start us, length us, event | category | flops | bytes accessed | tf_op | source)
XLA Modules:
  0.0 70.7 jit_solution(17669308462071811462)
XLA Ops:
  0.0 68.2 %ladder.1 = bf16[2500,256]{1,0:T(8,128)(2,1)} custom-call(bf16[40,2,2500]{2,1,0:T(2,128)(2,1)} %amp_ref.1, s32[1024]{0:T(1024)} %ab_ref.1, s32[1280]{0:T(1024)} %cd_ref.1, bf16[1024,1280]{1,0:T(8,128)(2,1)} %v_hbm.1), custom_call_target="tpu_custom_call" | custom-call | tf_op jit(solution)/shard_map/ladder/pallas_call | solution.py:522
  68.2 2.4 %copy.6 = bf16[256,2500]{0,1:T(8,128)(2,1)} copy(bf16[256,2500]{0,1:T(8,128)(2,1)} %bitcast.1) | data formatting | bytes 2560000

commit v7 on v6

--- a/solution.py
+++ b/solution.py
@@ -294,16 +294,17 @@
         ysend[n] = both[:OUT_ROWS]
         own[n] = both[OUT_ROWS:]
 
+    def core_arrive(n):
+        core_copy(n, 0).wait_recv()
+        core_copy(n, 1).wait_recv()
+
     def core_sum(n):
-        core_copy(n, 0).wait_recv()
         part = ysend[n] + crecv[n, 0]
         biggest = jnp.max(jnp.abs(part), axis=0, keepdims=True)
         ex = jnp.ceil(jnp.log2(jnp.maximum(biggest, 1e-30))) - 15.0
         q = jnp.clip(jnp.floor(part * jnp.exp2(-ex) + 0.5), -32767.0, 32767.0)
         ycode[n, :OUT_ROWS] = q.astype(jnp.int32).astype(jnp.int16)
         ycode[n, OUT_ROWS:] = jnp.broadcast_to(ex, (16, LANES)).astype(jnp.int32).astype(jnp.int16)
-        lo_copy(n).start()
-        core_copy(n, 1).wait_recv()
         own[n] += crecv[n, 1]
 
     def finish(n):
@@ -394,37 +395,47 @@
             def _():
                 forward(n, s)
 
-    def body(t, _):
-        @pl.when(t < FIRST)
-        def _():
-            event(2 * t)
-
+    def opening(t, _):
+        event(2 * t)
         arrive(t)
         expand(t)
         to_core(t)
-
-        @pl.when(t >= 1)
-        def _():
-            core_sum(t - 1)
-
+        event(2 * t + 1)
         keep(t)
-
-        @pl.when(t < FIRST)
-        def _():
-            event(2 * t + 1)
 
         @pl.when(t == 0)
         def _():
             for n in range(FULL, FIRST):
                 end_thin(n)
 
-        @pl.when(t >= 3)
-        def _():
-            finish(t - 3)
-
-        return 0
-
-    lax.fori_loop(0, CHUNKS, body, 0)
+        return 0
+
+    def body(t, _):
+        @pl.when(t < FIRST)
+        def _():
+            event(2 * t)
+
+        arrive(t)
+        expand(t)
+        to_core(t)
+
+        @pl.when(t < FIRST)
+        def _():
+            event(2 * t + 1)
+
+        core_arrive(t - 2)
+        core_sum(t - 2)
+        keep(t)
+        lo_copy(t - 2).start()
+
+        @pl.when(t >= 4)
+        def _():
+            finish(t - 4)
+
+        return 0
+
+    lax.fori_loop(0, 2, opening, 0)
+    lax.fori_loop(2, CHUNKS, body, 0)
 
     def finish_some(n, _):
         finish(n)
@@ -466,8 +477,14 @@
         mirror_copy(n).wait_send()
         return 0
 
-    core_sum(9)
-    lax.fori_loop(7, 9, finish_some, 0)
+    def last_sums(n, _):
+        core_arrive(n)
+        core_sum(n)
+        lo_copy(n).start()
+        return 0
+
+    lax.fori_loop(8, CHUNKS, last_sums, 0)
+    lax.fori_loop(6, 9, finish_some, 0)
     lax.fori_loop(0, CHUNKS, drain, 0)
     lax.fori_loop(0, 5, mirror_wait, 0)
     place_opposite()

time: 70.8 us -> 71.3 us (level); the launches traced: 70.7 us -> 70.2 us
  no operation moved by 1% of the time
where the time goes in v7:
time: 71.3 us; the launch traced here: 70.2 us
  Pallas kernels  67.7 us (95%)
  local copies, waits for them, and re-layouts  2.44 us (3%)
    pallas_call x1, Pallas kernels, local(): pl.pallas_call(kernel, out_shape=jax.ShapeDtypeStruct((OCC * SUB, OUT_ROW...  67.7 us
    unnamed x1, local copies, waits for them, and re-layouts  2.44 us

profile of v7, /device:TPU:1, one launch (start us, length us, event | category | flops | bytes accessed | tf_op | source)
XLA Modules:
  0.0 70.2 jit_solution(5862966960273520982)
XLA Ops:
  0.0 67.7 %ladder.1 = bf16[2500,256]{1,0:T(8,128)(2,1)} custom-call(bf16[40,2,2500]{2,1,0:T(2,128)(2,1)} %amp_ref.1, s32[1024]{0:T(1024)} %ab_ref.1, s32[1280]{0:T(1024)} %cd_ref.1, bf16[1024,1280]{1,0:T(8,128)(2,1)} %v_hbm.1), custom_call_target="tpu_custom_call" | custom-call | tf_op jit(solution)/shard_map/ladder/pallas_call | solution.py:539
  67.7 2.4 %copy.6 = bf16[256,2500]{0,1:T(8,128)(2,1)} copy(bf16[256,2500]{0,1:T(8,128)(2,1)} %bitcast.1) | data formatting | bytes 2560000

commit v8 on v7

--- a/solution.py
+++ b/solution.py
@@ -14,8 +14,14 @@
 CHUNKS = 10
 HALF = 640
 PAD = 15
-FIRST = 6
-LAST = CHUNKS - FIRST
+FIRST = 5
+EVENTS = {
+    (0, 0): [(5, 1), (6, 1), (7, 1)], (0, 1): [(8, 1), (9, 1)],
+    (2, 0): [(5, 2)], (2, 1): [(6, 2)], (2, 2): [(7, 2)],
+    (3, 1): [(8, 2)], (3, 2): [(9, 2)],
+    (4, 1): [(5, 3)], (4, 2): [(6, 3)],
+    (5, 0): [(7, 3)], (5, 1): [(8, 3)], (5, 2): [(9, 3)],
+}
 THIN = 3
 FULL = FIRST - THIN
 CUT = 48
@@ -334,7 +340,7 @@
         mine = r_own[0:5].reshape(HALF, OUT_ROWS)
         direct = mine.astype(jnp.float32)
         turned = dot(pt_ref[...], mine)
-        tmp_ref[...] = jnp.where(ib > ia, direct, jnp.where(ib < ia, -turned, 0.0))
+        tmp_ref[...] = jnp.where(ib > ia, direct, -turned)
         place(tmp_ref, 0)
         tmp_ref[...] = jnp.where(ib <= ia, direct, -dot(pt_ref[...], r_recv[0:5].reshape(HALF, OUT_ROWS)))
         place(tmp_ref, 2)
@@ -385,22 +391,23 @@
     lax.fori_loop(FULL, FIRST, middle_thin, 0)
     lax.fori_loop(0, FULL, late, 0)
     lax.fori_loop(FULL, FIRST, late_thin, 0)
-    part_start(CHUNKS - 1)
-
-    def event(i):
-        n = FIRST + i % LAST
-        for s in range(1, 4):
-
-            @pl.when(i // LAST == s - 1)
-            def _():
-                forward(n, s)
+    lax.fori_loop(FULL + FIRST, CHUNKS, first_part, 0)
+
+    def events(t, place, passes):
+        for at in passes:
+            if (at, place) in EVENTS:
+
+                @pl.when(t == at)
+                def _():
+                    for n, s in EVENTS[at, place]:
+                        forward(n, s)
 
     def opening(t, _):
-        event(2 * t)
+        events(t, 0, (0, 1))
         arrive(t)
         expand(t)
         to_core(t)
-        event(2 * t + 1)
+        events(t, 1, (0, 1))
         keep(t)
 
         @pl.when(t == 0)
@@ -411,22 +418,16 @@
         return 0
 
     def body(t, _):
-        @pl.when(t < FIRST)
-        def _():
-            event(2 * t)
-
+        events(t, 0, range(2, CHUNKS))
         arrive(t)
         expand(t)
         to_core(t)
-
-        @pl.when(t < FIRST)
-        def _():
-            event(2 * t + 1)
-
+        events(t, 1, range(2, CHUNKS))
         core_arrive(t - 2)
         core_sum(t - 2)
         keep(t)
         lo_copy(t - 2).start()
+        events(t, 2, range(2, CHUNKS))
 
         @pl.when(t >= 4)
         def _():
@@ -547,7 +548,10 @@
         ),
         name="ladder",
     )(amplitudes, ab_irrep, cd_irrep, integrals)
-    return turned.T
+    at = lax.broadcasted_iota(jnp.int32, turned.shape, 0)
+    i = (at * 5243) >> 19
+    same = at - OCC * i == i + SUB * lax.axis_index("col")
+    return jnp.where(same, jnp.zeros_like(turned), turned).T
 
 
 def solution(mesh):

time: 71.3 us -> 77.3 us (1.084)
  Pallas kernels: 67.7 us -> 72.9 us
  other arithmetic: 0 us -> 3.24 us
  local copies, waits for them, and re-layouts: 2.44 us -> 0 us
    pallas_call x1, Pallas kernels: 67.7 us -> 72.9 us  [local(): pl.pallas_call(kernel, out_shape=jax.ShapeDtypeStruct((OCC * SUB, OUT_ROW...]
    transpose x0 -> x1, other arithmetic: none -> 3.23 us  [local(): return jnp.where(same, jnp.zeros_like(turned), turned).T]
    unnamed x1 -> x0, local copies, waits for them, and re-layouts: 2.44 us -> none
where the time goes in v8:
time: 77.3 us; the launch traced here: 76.2 us
  Pallas kernels  72.9 us (94%)
  other arithmetic  3.24 us (4%)
    pallas_call x1, Pallas kernels, local(): pl.pallas_call(kernel, out_shape=jax.ShapeDtypeStruct((OCC * SUB, OUT_ROW...  72.9 us
    transpose x1, other arithmetic, local(): return jnp.where(same, jnp.zeros_like(turned), turned).T  3.23 us

profile of v8, /device:TPU:1, one launch (start us, length us, event | category | flops | bytes accessed | tf_op | source)
XLA Modules:
  0.0 76.2 jit_solution(16765743204065651732)
XLA Ops:
  0.0 72.9 %ladder.1 = bf16[2500,256]{1,0:T(8,128)(2,1)} custom-call(bf16[40,2,2500]{2,1,0:T(2,128)(2,1)} %amp_ref.1, s32[1024]{0:T(1024)} %ab_ref.1, s32[1280]{0:T(1024)} %cd_ref.1, bf16[1024,1280]{1,0:T(8,128)(2,1)} %v_hbm.1), custom_call_target="tpu_custom_call" | custom-call | tf_op jit(solution)/shard_map/ladder/pallas_call | solution.py:540
  73.0 3.2 %select_bitcast_fusion = bf16[256,2500]{0,1:T(8,128)(2,1)} fusion(bf16[2500,256]{1,0:T(8,128)(2,1)} %ladder.1, pred[2500]{0:T(1024)(128)(4,1)S(1)} %fusion.3), kind=kLoop, calls=%fused_computation | loop fusion | flops 640000 | bytes 2562500 | tf_op jit(solution)/shard_map/transpose | solution.py:554
  (1 shorter events, 0.0 us)

commit v9 on v7

--- a/solution.py
+++ b/solution.py
@@ -226,10 +226,6 @@
     lax.fori_loop(5, CHUNKS, own_start, 0)
     make_vp(3, 0)
 
-    def products(half):
-        both = dot(vp_ref[512 * half:512 * half + 512, :], bhl[...])
-        return both[:, :LANES] + both[:, LANES:]
-
     def part_start(n):
         hi_copy(n).wait_recv()
         start_both(first_copies(n, 1))
@@ -284,15 +280,14 @@
         bhl[:, :LANES] = (hi.astype(jnp.float32) * (s * 256.0)).astype(jnp.bfloat16)
         bhl[:, LANES:] = (lo.astype(jnp.float32) * s).astype(jnp.bfloat16)
 
-    def to_core(n):
-        csend[n] = products(0).reshape(2, OUT_ROWS, LANES)
+    def multiply(n):
+        both = dot(vp_ref[...], bhl[...])
+        both = both[:, :LANES] + both[:, LANES:]
+        csend[n] = both[:2 * OUT_ROWS].reshape(2, OUT_ROWS, LANES)
         core_copy(n, 0).start()
         core_copy(n, 1).start()
-
-    def keep(n):
-        both = products(1)
-        ysend[n] = both[:OUT_ROWS]
-        own[n] = both[OUT_ROWS:]
+        ysend[n] = both[2 * OUT_ROWS:3 * OUT_ROWS]
+        own[n] = both[3 * OUT_ROWS:]
 
     def core_arrive(n):
         core_copy(n, 0).wait_recv()
@@ -399,9 +394,8 @@
         event(2 * t)
         arrive(t)
         expand(t)
-        to_core(t)
+        multiply(t)
         event(2 * t + 1)
-        keep(t)
 
         @pl.when(t == 0)
         def _():
@@ -417,7 +411,7 @@
 
         arrive(t)
         expand(t)
-        to_core(t)
+        multiply(t)
 
         @pl.when(t < FIRST)
         def _():
@@ -425,7 +419,6 @@
 
         core_arrive(t - 2)
         core_sum(t - 2)
-        keep(t)
         lo_copy(t - 2).start()
 
         @pl.when(t >= 4)

time: 71.3 us -> 68.4 us (0.959)
  Pallas kernels: 67.7 us -> 65.4 us
    pallas_call x1, Pallas kernels: 67.7 us -> 65.4 us  [local(): pl.pallas_call(kernel, out_shape=jax.ShapeDtypeStruct((OCC * SUB, OUT_ROW...]
where the time goes in v9:
time: 68.4 us; the launch traced here: 67.8 us
  Pallas kernels  65.4 us (96%)
  local copies, waits for them, and re-layouts  2.44 us (4%)
    pallas_call x1, Pallas kernels, local(): pl.pallas_call(kernel, out_shape=jax.ShapeDtypeStruct((OCC * SUB, OUT_ROW...  65.4 us
    unnamed x1, local copies, waits for them, and re-layouts  2.44 us

profile of v9, /device:TPU:1, one launch (start us, length us, event | category | flops | bytes accessed | tf_op | source)
XLA Modules:
  0.0 67.8 jit_solution(1703082575632757599)
XLA Ops:
  0.0 65.4 %ladder.1 = bf16[2500,256]{1,0:T(8,128)(2,1)} custom-call(bf16[40,2,2500]{2,1,0:T(2,128)(2,1)} %amp_ref.1, s32[1024]{0:T(1024)} %ab_ref.1, s32[1280]{0:T(1024)} %cd_ref.1, bf16[1024,1280]{1,0:T(8,128)(2,1)} %v_hbm.1), custom_call_target="tpu_custom_call" | custom-call | tf_op jit(solution)/shard_map/ladder/pallas_call | solution.py:532
  65.4 2.4 %copy.6 = bf16[256,2500]{0,1:T(8,128)(2,1)} copy(bf16[256,2500]{0,1:T(8,128)(2,1)} %bitcast.1) | data formatting | bytes 2560000

commit v10 on v9

--- a/solution.py
+++ b/solution.py
@@ -52,10 +52,10 @@
 
 
 def kernel(
-    amp_ref, ab_ref, cd_ref, v_hbm, out_ref,
-    t_ref, v_ref, vp_ref, pk_ref, pt_ref, x_ref, diag_ref, wsend, wrecv, bq, sc_ref, bhl,
+    amp_hbm, ab_ref, cd_ref, v_hbm, out_ref,
+    amp_ref, t_ref, v_ref, vp_ref, pk_ref, pt_ref, x_ref, diag_ref, wsend, wrecv, bq, sc_ref, bhl,
     csend, crecv, ysend, ycode, yrecv, own, r_own, r_recv, tmp_ref, acc_ref,
-    v_sem, w_ss, w_rs, h_ss, h_rs, t_ss, t_rs, zr_ss, zr_rs, zl_ss, zl_rs, c_ss, c_rs, y_ss, y_rs, m_ss, m_rs,
+    a_sem, v_sem, w_ss, w_rs, h_ss, h_rs, t_ss, t_rs, zr_ss, zr_rs, zl_ss, zl_rs, c_ss, c_rs, y_ss, y_rs, m_ss, m_rs,
 ):
     row, c, depth = lax.axis_index("row"), lax.axis_index("col"), lax.axis_index("depth")
     z, yh = row // 2, row % 2
@@ -74,15 +74,12 @@
             src_ref=src, dst_ref=dst, send_sem=ss, recv_sem=rs, device_id=dev, device_id_type=MESH
         )
 
-    v_copy = pltpu.make_async_copy(v_hbm, v_ref, v_sem)
-    v_copy.start()
+    a_copy = pltpu.make_async_copy(amp_hbm, amp_ref, a_sem)
+    a_copy.start()
 
     barrier = pltpu.get_barrier_semaphore()
     for dev in (d_right, d_left, d_hi, d_core, d_lo, x_next, x_opp, x_prev):
         pl.semaphore_signal(barrier, inc=1, device_id=dev, device_id_type=MESH)
-
-    t_ref[:, 2432:] = jnp.zeros((ROWS_T, LANES), jnp.bfloat16)
-    t_ref[:, : OCC * SUB] = amp_ref[...].reshape(ROWS_T, OCC * SUB)
 
     u = iota((1, HALF), 1) - PAD
     a = div25(u)
@@ -90,6 +87,12 @@
     flip = jnp.where(u >= 0, PAD + SUB * b + a, -1)
     lower = b <= a
     pt_ref[...] = one_hot(iota((HALF, HALF), 0) == flip)
+
+    a_copy.wait()
+    v_copy = pltpu.make_async_copy(v_hbm, v_ref, v_sem)
+    v_copy.start()
+    t_ref[:, 2432:] = jnp.zeros((ROWS_T, LANES), jnp.bfloat16)
+    t_ref[:, : OCC * SUB] = amp_ref[...].reshape(ROWS_T, OCC * SUB)
 
     for n in range(HALF // LANES):
         low, high = band(n)
@@ -106,11 +109,12 @@
             x_ref[g, :, n * LANES:(n + 1) * LANES] = got[:, g * LANES:(g + 1) * LANES]
 
     wsend[1] = dot(x_ref[2], pt_ref[...]).astype(jnp.bfloat16)
+    wsend[0] = dot(x_ref[3], pt_ref[...]).astype(jnp.bfloat16)
     pl.semaphore_wait(barrier, 8)
     w0 = copy(wsend.at[0], wrecv.at[0], w_ss.at[0], w_rs.at[0], x_prev)
     w1 = copy(wsend.at[1], wrecv.at[1], w_ss.at[1], w_rs.at[1], x_opp)
     w1.start()
-    wsend[0] = dot(x_ref[3], pt_ref[...]).astype(jnp.bfloat16)
+    w0.start()
     x0 = x_ref[0]
     diag_ref[...] = x0.astype(jnp.float32) - dot(x0, pt_ref[...])
 
@@ -127,8 +131,6 @@
         return 0
 
     lax.fori_loop(0, DEPTH // 256, make_pk, 0)
-    w1.wait_send()
-    w0.start()
     v_copy.wait()
 
     def make_vp(i, _):
@@ -141,7 +143,6 @@
         vp_ref[pl.ds(pl.multiple_of(to, 128), 128), :] = dot(masked, pk_ref[...]).astype(jnp.bfloat16)
         return 0
 
-    lax.fori_loop(0, 2, make_vp, 0)
 
     def encode(values, chunk):
         biggest = jnp.max(jnp.abs(values), axis=1, keepdims=True)
@@ -220,7 +221,7 @@
     opposite = x_ref[2].astype(jnp.float32) - wrecv[1].astype(jnp.float32)
     encode(jnp.where(lower, opposite, diag_ref[...]), 0)
     lax.fori_loop(0, 5, own_start, 0)
-    make_vp(2, 0)
+    lax.fori_loop(0, 3, make_vp, 0)
     w0.wait_recv()
     encode(x_ref[1].astype(jnp.float32) - wrecv[0].astype(jnp.float32), 5)
     lax.fori_loop(5, CHUNKS, own_start, 0)
@@ -421,9 +422,9 @@
         core_sum(t - 2)
         lo_copy(t - 2).start()
 
-        @pl.when(t >= 4)
-        def _():
-            finish(t - 4)
+        @pl.when(t >= 5)
+        def _():
+            finish(t - 5)
 
         return 0
 
@@ -477,12 +478,13 @@
         return 0
 
     lax.fori_loop(8, CHUNKS, last_sums, 0)
-    lax.fori_loop(6, 9, finish_some, 0)
+    lax.fori_loop(5, 9, finish_some, 0)
     lax.fori_loop(0, CHUNKS, drain, 0)
     lax.fori_loop(0, 5, mirror_wait, 0)
     place_opposite()
     finish(9)
     w0.wait_send()
+    w1.wait_send()
     lax.fori_loop(0, CHUNKS, drain_sums, 0)
     place_next()
     lax.fori_loop(5, CHUNKS, mirror_wait, 0)
@@ -497,6 +499,7 @@
     dma = pltpu.SemaphoreType.DMA
     n = CHUNKS
     scratch = [
+        pltpu.VMEM((40, 2, OCC * SUB), bf),
         pltpu.VMEM((ROWS_T, WIDE), bf),
         pltpu.VMEM((1024, DEPTH), bf),
         pltpu.VMEM((1024, DEPTH), bf),
@@ -520,6 +523,7 @@
         pltpu.VMEM((HALF, OUT_ROWS), f32),
         pltpu.VMEM((OCC * SUB, OUT_ROWS), f32),
         dma,
+        dma,
         dma((2,)), dma((2,)),
         dma((n,)), dma((n,)),
         dma((THIN, 7)), dma((THIN, 7)),
@@ -532,7 +536,7 @@
     turned = pl.pallas_call(
         kernel,
         out_shape=jax.ShapeDtypeStruct((OCC * SUB, OUT_ROWS), bf),
-        in_specs=[vmem, vmem, vmem, pl.BlockSpec(memory_space=pl.ANY)],
+        in_specs=[pl.BlockSpec(memory_space=pl.ANY), vmem, vmem, pl.BlockSpec(memory_space=pl.ANY)],
         out_specs=vmem,
         scratch_shapes=scratch,
         compiler_params=pltpu.CompilerParams(

time: 68.4 us -> 68.6 us (level)
  no operation moved by 1% of the time
where the time goes in v10:
time: 68.6 us; the launch traced here: 68.4 us
  Pallas kernels  65.9 us (96%)
  local copies, waits for them, and re-layouts  2.44 us (4%)
    pallas_call x1, Pallas kernels, local(): pl.pallas_call(kernel, out_shape=jax.ShapeDtypeStruct((OCC * SUB, OUT_ROW...  65.9 us
    unnamed x1, local copies, waits for them, and re-layouts  2.44 us

profile of v10, /device:TPU:1, one launch (start us, length us, event | category | flops | bytes accessed | tf_op | source)
XLA Modules:
  0.0 68.4 jit_solution(15946106060698482263)
XLA Ops:
  0.0 65.9 %ladder.1 = bf16[2500,256]{1,0:T(8,128)(2,1)} custom-call(bf16[40,2,2500]{2,1,0:T(2,128)(2,1)} %amp_hbm.1, s32[1024]{0:T(1024)} %ab_ref.1, s32[1280]{0:T(1024)} %cd_ref.1, bf16[1024,1280]{1,0:T(8,128)(2,1)} %v_hbm.1), custom_call_target="tpu_custom_call" | custom-call | tf_op jit(solution)/shard_map/ladder/pallas_call | solution.py:536
  65.9 2.4 %copy.6 = bf16[256,2500]{0,1:T(8,128)(2,1)} copy(bf16[256,2500]{0,1:T(8,128)(2,1)} %bitcast.1) | data formatting | bytes 2560000

commit v11 on v9

--- a/solution.py
+++ b/solution.py
@@ -421,9 +421,9 @@
         core_sum(t - 2)
         lo_copy(t - 2).start()
 
-        @pl.when(t >= 4)
-        def _():
-            finish(t - 4)
+        @pl.when(t >= 5)
+        def _():
+            finish(t - 5)
 
         return 0
 
@@ -477,7 +477,7 @@
         return 0
 
     lax.fori_loop(8, CHUNKS, last_sums, 0)
-    lax.fori_loop(6, 9, finish_some, 0)
+    lax.fori_loop(5, 9, finish_some, 0)
     lax.fori_loop(0, CHUNKS, drain, 0)
     lax.fori_loop(0, 5, mirror_wait, 0)
     place_opposite()

time: 68.4 us -> 68.2 us (level)
  no operation moved by 1% of the time
where the time goes in v11:
time: 68.2 us; the launch traced here: 68 us
  Pallas kernels  65.6 us (96%)
  local copies, waits for them, and re-layouts  2.44 us (4%)
    pallas_call x1, Pallas kernels, local(): pl.pallas_call(kernel, out_shape=jax.ShapeDtypeStruct((OCC * SUB, OUT_ROW...  65.6 us
    unnamed x1, local copies, waits for them, and re-layouts  2.44 us

profile of v11, /device:TPU:1, one launch (start us, length us, event | category | flops | bytes accessed | tf_op | source)
XLA Modules:
  0.0 68.0 jit_solution(4861083831078402615)
XLA Ops:
  0.0 65.6 %ladder.1 = bf16[2500,256]{1,0:T(8,128)(2,1)} custom-call(bf16[40,2,2500]{2,1,0:T(2,128)(2,1)} %amp_ref.1, s32[1024]{0:T(1024)} %ab_ref.1, s32[1280]{0:T(1024)} %cd_ref.1, bf16[1024,1280]{1,0:T(8,128)(2,1)} %v_hbm.1), custom_call_target="tpu_custom_call" | custom-call | tf_op jit(solution)/shard_map/ladder/pallas_call | solution.py:532
  65.6 2.4 %copy.6 = bf16[256,2500]{0,1:T(8,128)(2,1)} copy(bf16[256,2500]{0,1:T(8,128)(2,1)} %bitcast.1) | data formatting | bytes 2560000
